TPU v7x, 32 devices: a whole 2x2x4 slice. The times are simulated.
32 devices in a mesh: group: 2 (over y), request: 4 (over z), tensor: 4 (over x, core).
Axes of the slice: x: 2, y: 2, z: 4, core: 2. Of those that a mesh axis runs over, the one named last changes fastest.
Arguments:
- queries: bfloat16 [8, 384, 8192], P(('group', 'request'), 'tensor'), parts along dimension 0, may hold values from -30 to 30
- kv_new: bfloat16 [8, 384, 2048], P(('group', 'request'), 'tensor'), parts along dimension 0, may hold values from -8 to 8
- pool: bfloat16 [8, 4, 128, 2048], P(('group', 'request'), None, None, 'tensor'), parts along dimension 0, may hold values from -16 to 16
- counts: int32 [8], P('group'), parts along dimension 0, may hold values from 1 to 4, 8 in all
- holder_map: int32 [8, 4], P('group'), parts along dimension 0, may hold values from 0 to 3, each once within a row
Outputs:
- attended: bfloat16 [8, 384, 8192], P(('group', 'request'), 'tensor'), parts along dimension 0
There are 2 independent parts, one for each index of `group`. A program takes and returns all parts, laid end to end along the dimension named above; each array names one. Nothing has to cross between parts.
Inputs may be any that keep to these rules, and one draw needn't show every extreme that they name: Stored span counts; some request has exactly 4. `holder_map`: each row names every rank once.
All inputs are finite; a program needn't handle non-finite values.
Results may differ from a plain program's by a relative error of at most 0.003.
Values may be sent and summed in bfloat16 or wider, within the bound.
No kernel may reach another device: no remote copies, remote signals or barrier semaphores. Data moves between devices by JAX's collectives and lax.ppermute only.
A program may use at most 64 MiB of HBM per device.

v0:
```python
import jax
import jax.numpy as jnp
from jax import lax
from jax.sharding import PartitionSpec as P

HD = 128


def causal_mask(rows, cols):
    return lax.broadcasted_iota(jnp.int32, (rows, cols), 0) >= lax.broadcasted_iota(
        jnp.int32, (rows, cols), 1
    )


def attend_joint(query, keys_all, values_all, visible):
    scale = query.shape[-1] ** (-0.5)
    scores = jnp.dot(query, keys_all.T, preferred_element_type=jnp.float32) * scale
    scores = jnp.where(visible, scores, -jnp.inf)
    peak = jnp.max(scores, axis=1)[:, None]
    weights = jnp.where(visible, jnp.exp(scores - peak), 0.0)
    total = jnp.sum(weights, axis=1)
    acc = jnp.dot(weights.astype(jnp.bfloat16), values_all, preferred_element_type=jnp.float32)
    return (acc / total[:, None]).astype(jnp.bfloat16)


def local(queries, kv_new, pool, counts, holder_map):
    head_q, head_kv = (
        lax.all_to_all(queries, "tensor", split_axis=2, concat_axis=1, tiled=True),
        lax.all_to_all(kv_new, "tensor", split_axis=2, concat_axis=1, tiled=True),
    )
    stored = lax.all_to_all(pool, "request", split_axis=1, concat_axis=0, tiled=True)
    tokens_new = head_q.shape[1]
    local_heads = head_q.shape[2] // HD
    local_kv = head_kv.shape[2] // (2 * HD)
    group_size = local_heads // local_kv
    holders = stored.shape[0]
    span = stored.shape[2]
    me = lax.axis_index("request")
    count = lax.dynamic_index_in_dim(counts, me, 0, keepdims=False)
    row = lax.dynamic_index_in_dim(holder_map, me, 0, keepdims=False)
    q_local = head_q[0].reshape(tokens_new, local_heads, HD).transpose(1, 0, 2)
    own = head_kv[0].reshape(tokens_new, local_kv, 2, HD)
    outputs = []
    ranks = jnp.arange(holders, dtype=jnp.int32)
    hits = (row[:, None] == ranks[None, :]) & (ranks[:, None] < count)
    valid = jnp.sum(hits.astype(jnp.int32), axis=0) > 0
    live = jnp.repeat(valid, span)
    flat = stored[:, 0].reshape(holders * span, local_kv, 2, HD)
    for kv_head in range(local_kv):
        q_group = q_local[kv_head * group_size : (kv_head + 1) * group_size]
        keys_own = own[:, kv_head, 0]
        values_own = own[:, kv_head, 1]
        keys_st = flat[:, kv_head, 0]
        values_st = flat[:, kv_head, 1]
        keys_all = jnp.concatenate([keys_st, keys_own], axis=0)
        values_all = jnp.concatenate([values_st, values_own], axis=0)
        causal = causal_mask(tokens_new, tokens_new)
        visible = jnp.concatenate(
            [jnp.broadcast_to(live[None, :], (tokens_new, live.shape[0])), causal], axis=1
        )
        outputs.append(
            lax.map(lambda query: attend_joint(query, keys_all, values_all, visible), q_group)
        )
    heads_out = jnp.concatenate(outputs, axis=0)
    result = heads_out.transpose(1, 0, 2).reshape(1, tokens_new, local_heads * HD)
    return lax.all_to_all(result, "tensor", split_axis=1, concat_axis=2, tiled=True)


def solution(mesh):
    placed = (
        P(("group", "request"), "tensor", None),
        P(("group", "request"), "tensor", None),
        P(("group", "request"), None, None, "tensor"),
        P("group"),
        P("group", None),
    )
    return jax.shard_map(
        local,
        mesh=mesh,
        in_specs=placed,
        out_specs=P(("group", "request"), "tensor", None),
        check_vma=False,
    )
```

profile of v0, /device:TPU:0, one launch (start us, length us, event | category | flops | bytes accessed | tf_op | source)
XLA Modules:
  0.0 223.7 jit_solution(3763486009300142068)
XLA Ops:
  0.0 2.3 %copy.65 = bf16[1,96,2048]{1,0,2:T(2,128)(2,1)S(1)} copy(bf16[1,96,2048]{2,1,0:T(8,128)(2,1)} %param.10) | data formatting | bytes 786432 | tf_op args[1]
  2.9 11.5 %reduce.1 = bf16[2048,96]{1,0:T(8,128)(2,1)S(1)} reduce(bf16[2048,1,96]{2,1,0:T(2,128)(2,1)S(1)} %bitcast.95, bf16[]{:T(256)} %broadcast.28), dimensions={1}, to_apply=%bitcast.56.reduce_sub_computation | reduce | bytes 786434
  14.5 1.6 reshape.25
  16.1 4.2 %all-to-all-start.2 = ((bf16[4,2,24576]{2,1,0:T(2,128)(2,1)}), bf16[4,2,24576]{2,1,0:T(2,128)(2,1)S(1)}, u32[]{:S(2)}, u32[]{:S(2)}) async-start(bf16[4,2,24576]{2,1,0:T(2,128)(2,1)} %reshape.25), calls=%async_computation.2 | async-start | bytes 786432 | tf_op jit(solution)/shard_map/all_to_all | solution.py:29
  20.9 0.6 iota_compare_fusion.2
  21.6 9.4 %copy.61 = bf16[1,96,8192]{1,0,2:T(2,128)(2,1)} copy(bf16[1,96,8192]{2,1,0:T(8,128)(2,1)} %param.9) | data formatting | bytes 3145728 | tf_op args[0]
  31.0 45.2 %reduce = bf16[8192,96]{1,0:T(8,128)(2,1)S(1)} reduce(bf16[8192,1,96]{2,1,0:T(2,128)(2,1)} %bitcast.87, bf16[]{:T(256)} %broadcast.28), dimensions={1}, to_apply=%bitcast.54.reduce_sub_computation | reduce | bytes 3145730
  76.2 4.1 %reshape.23 = bf16[4,2,98304]{2,1,0:T(2,128)(2,1)} reshape(bf16[8192,96]{1,0:T(8,128)(2,1)S(1)} %reduce) | data formatting | bytes 3145728
  80.4 5.8 %all-to-all-start.1 = ((bf16[1,4,128,512]{3,2,0,1:T(8,128)(2,1)}), bf16[1,4,128,512]{3,2,0,1:T(8,128)(2,1)S(1)}, u32[]{:S(2)}, u32[]{:S(2)}) async-start(bf16[1,4,128,512]{3,2,0,1:T(8,128)(2,1)} %bitcast.98), calls=%async_computation.1 | async-start | bytes 1048576 | tf_op jit(solution)/shard_map/all_to_all | solution.py:31
  86.3 0.8 reshape.26
  90.1 0.7 copy_bitcast_fusion.5
  90.7 10.3 %all-to-all-done.1 = bf16[1,4,128,512]{3,2,0,1:T(8,128)(2,1)S(1)} async-done(((bf16[1,4,128,512]{3,2,0,1:T(8,128)(2,1)}), bf16[1,4,128,512]{3,2,0,1:T(8,128)(2,1)S(1)}, u32[]{:S(2)}, u32[]{:S(2)}) %all-to-all-start.1) | async-done | bytes 524320 | tf_op jit(solution)/shard_map/all_to_all | solution.py:31
  101.1 3.8 %all-to-all-start = ((bf16[4,2,98304]{2,1,0:T(2,128)(2,1)}), bf16[4,2,98304]{2,1,0:T(2,128)(2,1)S(1)}, u32[]{:S(2)}, u32[]{:S(2)}) async-start(bf16[4,2,98304]{2,1,0:T(2,128)(2,1)} %reshape.23), calls=%async_computation | async-start | bytes 3145728 | tf_op jit(solution)/shard_map/all_to_all | solution.py:28
  105.0 0.7 fusion.28
  105.9 0.7 pad_maximum_fusion.4
  106.7 0.7 pad_maximum_fusion.2
  107.4 17.3 %all-to-all-done = bf16[4,2,98304]{2,1,0:T(2,128)(2,1)S(1)} async-done(((bf16[4,2,98304]{2,1,0:T(2,128)(2,1)}), bf16[4,2,98304]{2,1,0:T(2,128)(2,1)S(1)}, u32[]{:S(2)}, u32[]{:S(2)}) %all-to-all-start) | async-done | bytes 1572896 | tf_op jit(solution)/shard_map/all_to_all | solution.py:28
  124.7 4.2 %reshape.24 = bf16[8192,1,96]{2,1,0:T(2,128)(2,1)} reshape(bf16[4,2,98304]{2,1,0:T(2,128)(2,1)S(1)} %all-to-all-done) | data formatting | bytes 3145728
  128.9 9.0 %copy.62 = bf16[1,96,8192]{2,1,0:T(8,128)(2,1)} copy(bf16[1,96,8192]{1,0,2:T(2,128)(2,1)} %bitcast.86) | data formatting | bytes 3145728 | tf_op jit(solution)/shard_map/all_to_all | solution.py:28
  137.9 2.9 %all_to_all.43 = bf16[1,96,4,2048]{3,2,1,0:T(4,128)(2,1)S(1)} reshape(bf16[1,96,8192]{2,1,0:T(8,128)(2,1)} %copy.62) | data formatting | bytes 3145728 | tf_op jit(solution)/shard_map/all_to_all | solution.py:28
  140.8 0.9 copy.63
  142.4 16.4 %while.21 = (s32[]{:T(128)}, bf16[8,384,128]{1,2,0:T(8,128)(2,1)S(1)}, bf16[8,384,128]{2,1,0:T(8,128)(2,1)S(1)}, bf16[896,128]{1,0:T(8,128)(2,1)S(1)}, pred[384,...) while((s32[]{:T(128)}, bf16[8,384,128]{1,2,0:T(8,128)(2,1)S(1)}, ...), condition=%wide.region_8.9_spmd, body=%wide.region_5.8_spmd.sunk | while | flops 179354880 | bytes 7134841 | solution.py:62
  159.0 0.7 copy-done.4
  159.8 12.9 %while.20 = (s32[]{:T(128)}, bf16[8,384,128]{1,2,0:T(8,128)(2,1)S(1)}, bf16[8,384,128]{2,1,0:T(8,128)(2,1)S(1)}, bf16[896,128]{1,0:T(8,128)(2,1)S(1)}, pred[384,...) while((s32[]{:T(128)}, bf16[8,384,128]{1,2,0:T(8,128)(2,1)S(1)}, ...), condition=%wide.region_4.5_spmd, body=%wide.region_1.4_spmd.sunk | while | flops 179354880 | bytes 6217309 | solution.py:62
  172.6 1.3 pad_maximum_fusion
  173.9 7.3 %copy.73 = bf16[1,384,2048]{2,0,1:T(2,128)(2,1)S(1)} copy(bf16[1,384,2048]{1,2,0:T(8,128)(2,1)} %bitcast.93) | data formatting | bytes 3145728 | tf_op jit(solution)/shard_map/reshape | solution.py:65
  181.2 11.0 %reduce.2 = bf16[384,2048]{1,0:T(8,128)(2,1)} reduce(bf16[384,1,2048]{2,1,0:T(2,128)(2,1)S(1)} %bitcast.88, bf16[]{:T(256)} %broadcast.28), dimensions={1}, to_apply=%bitcast.58.reduce_sub_computation | reduce | bytes 3145730
  192.2 2.9 %reshape.27 = bf16[4,2,98304]{2,1,0:T(2,128)(2,1)S(1)} reshape(bf16[384,2048]{1,0:T(8,128)(2,1)} %reduce.2) | data formatting | bytes 3145728
  195.2 23.3 %all_to_all.57 = bf16[4,2,98304]{2,1,0:T(2,128)(2,1)} all-to-all(bf16[4,2,98304]{2,1,0:T(2,128)(2,1)S(1)} %reshape.27), channel_id=1, replica_groups=mesh['group'=2,'request'=4,'tensor'=4] {'tensor'}, dimensions={0} | all-to-all | bytes 3145728 | tf_op jit(solution)/shard_map/all_to_all | solution.py:66
  218.4 3.1 %reshape.28 = bf16[384,1,2048]{2,1,0:T(2,128)(2,1)S(1)} reshape(bf16[4,2,98304]{2,1,0:T(2,128)(2,1)} %all_to_all.57) | data formatting | bytes 3145728
  221.5 0.9 copy.86
  222.4 1.2 copy.88
  (135 shorter events, 34.4 us)
Async XLA Ops:
  0.0 20.3 %copy-start = (s32[4,4]{1,0:T(4,128)S(1)}, s32[4,4]{1,0:T(4,128)}, u32[]{:S(2)}) copy-start(s32[4,4]{1,0:T(4,128)} %param.13) | copy-start | bytes 196
  2.9 17.4 %copy-start.6 = (s32[4]{0:T(128)S(1)}, s32[4]{0:T(128)}, u32[]{:S(2)}) copy-start(s32[4]{0:T(128)} %param.12) | copy-start | bytes 52
  16.1 64.3 %all-to-all-start.2 = ((bf16[4,2,24576]{2,1,0:T(2,128)(2,1)}), bf16[4,2,24576]{2,1,0:T(2,128)(2,1)S(1)}, u32[]{:S(2)}, u32[]{:S(2)}) async-start(bf16[4,2,24576]{2,1,0:T(2,128)(2,1)} %reshape.25), calls=%async_computation.2 | async-start | bytes 786432 | tf_op jit(solution)/shard_map/all_to_all | solution.py:29
  80.4 20.7 %all-to-all-start.1 = ((bf16[1,4,128,512]{3,2,0,1:T(8,128)(2,1)}), bf16[1,4,128,512]{3,2,0,1:T(8,128)(2,1)S(1)}, u32[]{:S(2)}, u32[]{:S(2)}) async-start(bf16[1,4,128,512]{3,2,0,1:T(8,128)(2,1)} %bitcast.98), calls=%async_computation.1 | async-start | bytes 1048576 | tf_op jit(solution)/shard_map/all_to_all | solution.py:31
  101.1 23.6 %all-to-all-start = ((bf16[4,2,98304]{2,1,0:T(2,128)(2,1)}), bf16[4,2,98304]{2,1,0:T(2,128)(2,1)S(1)}, u32[]{:S(2)}, u32[]{:S(2)}) async-start(bf16[4,2,98304]{2,1,0:T(2,128)(2,1)} %reshape.23), calls=%async_computation | async-start | bytes 3145728 | tf_op jit(solution)/shard_map/all_to_all | solution.py:28
  105.0 0.9 copy-start.1
  105.7 0.9 copy-start.3
  105.7 0.9 copy-start.2
  142.9 0.9 copy-start.5
  144.9 0.9 copy-start.5
  147.0 0.9 copy-start.5
  149.0 0.9 copy-start.5
  151.1 0.9 copy-start.5
  153.1 0.9 copy-start.5
  155.2 0.9 copy-start.5
  157.2 0.9 copy-start.5
  158.8 0.9 copy-start.4
where the time goes:
time: 225 us; the launch traced here: 224 us
  other arithmetic  79.2 us (35%)
  local copies, waits for them, and re-layouts  64 us (28%)
  waiting for transfers between devices  27.6 us (12%)
  blocking collectives  23.3 us (10%)
  matrix products  15 us (7%)
  starting transfers between devices  13.8 us (6%)
    unnamed x3, other arithmetic  67.8 us
    unnamed x28, local copies, waits for them, and re-layouts  33.1 us
    all_to_all x1, blocking collectives, local(): lax.all_to_all(result, 'tensor', split_axis=1, concat_axis=2, tiled=True)  23.3 us
    all_to_all x1, waiting for transfers between devices, local(): lax.all_to_all(queries, 'tensor', split_axis=2, concat_axis=1, tiled=True)  17.3 us
    all_to_all x3, local copies, waits for them, and re-layouts, local(): lax.all_to_all(queries, 'tensor', split_axis=2, concat_axis=1, tiled=True)  12.8 us
    all_to_all x1, waiting for transfers between devices, local(): lax.all_to_all(pool, 'request', split_axis=1, concat_axis=0, tiled=True)  10.3 us
    reduce_sum x16, other arithmetic, attend_joint(): total = jnp.sum(weights, axis=1)  7.73 us
    dot_general x16, matrix products, attend_joint(): jnp.dot(weights.astype(jnp.bfloat16), values_all, preferred_element_type=...  7.51 us
  transfers between devices with their start and end apart: 3, of which 2 were waited for; matrix products, arithmetic and copies ran while one was open for 30% of the time, Pallas kernels for 0%

commit v1 on v0

v1 whole, which is shorter than its diff:
```python
import functools
import math

import jax
import jax.numpy as jnp
from jax import lax
from jax.experimental import pallas as pl
from jax.experimental.pallas import tpu as pltpu
from jax.sharding import PartitionSpec as P

HD = 128
NEG = -math.inf
TO_EXP2 = HD**-0.5 * math.log2(math.e)


def hop(piece, size, distance, bit, causal):
    pairs = [
        (i, i ^ bit) for i in range(size) if not causal or (i ^ distance) < (i ^ bit)
    ]
    return lax.ppermute(piece, "tensor", pairs)


def gather_by_distance(piece, size, causal=False):
    held = {0: piece}
    bit = size // 2
    while bit:
        for distance in sorted(held):
            held[distance + bit] = hop(held[distance], size, distance, bit, causal)
        bit //= 2
    return [held[d] for d in range(size)]


def attend_kernel(size, groups, heads, meta, *refs):
    q_ref, new, stored, o_ref = refs[0], refs[1 : 1 + size], refs[1 + size : -1], refs[-1]
    parts = [stored[d * groups : (d + 1) * groups] for d in range(size)]
    me = meta[0]
    tokens = q_ref.shape[0]
    span = stored[0].shape[1]
    spans = sum(part.shape[0] for part in parts[0])
    local_kv = new[0].shape[1] // (2 * HD) // size
    fresh = size * tokens
    keys = fresh + spans * span

    column = lax.broadcasted_iota(jnp.int32, (1, keys), 1)
    bias = jnp.zeros((1, keys), jnp.float32)
    for d in range(1, size):
        hidden = jnp.bitwise_xor(me, d) > me
        here = (column >= tokens * d) & (column < tokens * (d + 1))
        bias = jnp.where(here & hidden, NEG, bias)
    for s in range(spans):
        here = (column >= fresh + s * span) & (column < fresh + (s + 1) * span)
        bias = jnp.where(here & (meta[1 + s] == 0), NEG, bias)
    lead = -(-tokens // HD) * HD
    rows = lax.broadcasted_iota(jnp.int32, (tokens, lead), 0)
    cols = lax.broadcasted_iota(jnp.int32, (tokens, lead), 1)
    lead_bias = jnp.where((rows < cols) & (cols < tokens), NEG, bias[:, :lead])
    ones = jnp.ones((keys, HD), jnp.bfloat16)

    def columns(at, width=HD):
        return pl.ds(pl.multiple_of(at, HD), width)

    def side(d, i, which):
        head = jnp.bitwise_xor(me, d) * local_kv + i
        blocks = [ref[:, columns((2 * head + which) * HD)] for ref in new]
        at = (2 * i + which) * HD
        blocks += [
            part[s, :, at : at + HD] for part in parts[d] for s in range(part.shape[0])
        ]
        return jnp.concatenate(blocks, axis=0)

    def query_columns(d, i, h):
        head = jnp.bitwise_xor(me, d) * local_kv + i
        return columns((head * heads + h) * HD)

    def scores_of(d, i):
        query = jnp.concatenate([q_ref[:, query_columns(d, i, h)] for h in range(heads)], axis=0)
        return lax.dot_general(
            query, side(d, i, 0), (((1,), (1,)), ((), ())), preferred_element_type=jnp.float32
        )

    def finish(d, i, scores):
        value = jnp.concatenate([side(d, i, 1), ones], axis=1)
        scores = scores.reshape(heads, tokens, keys)
        scores = jnp.concatenate(
            [scores[:, :, :lead] + lead_bias[None], scores[:, :, lead:] + bias[:, lead:][None]],
            axis=2,
        ).reshape(heads * tokens, keys)
        peak = jnp.max(scores, axis=1, keepdims=True)
        weights = jnp.exp2((scores - peak) * TO_EXP2).astype(jnp.bfloat16)
        sums = jnp.dot(weights, value, preferred_element_type=jnp.float32)
        out = (sums[:, :HD] / sums[:, HD:]).astype(jnp.bfloat16)
        for h in range(heads):
            o_ref[:, query_columns(d, i, h)] = out[h * tokens : (h + 1) * tokens]

    order = [(d, i) for d in range(size) for i in range(local_kv)]
    scores = scores_of(*order[0])
    for n, at in enumerate(order):
        later = scores_of(*order[n + 1]) if n + 1 < len(order) else None
        finish(*at, scores)
        scores = later


def attend(meta, query, new, stored):
    size = len(new)
    groups = len(stored[0])
    heads = query.shape[1] // new[0].shape[1] * 2
    whole = pl.BlockSpec(memory_space=pltpu.VMEM)
    operands = [query, *new, *(part for parts in stored for part in parts)]
    return pl.pallas_call(
        functools.partial(attend_kernel, size, groups, heads),
        out_shape=jax.ShapeDtypeStruct(query.shape, query.dtype),
        in_specs=[pl.BlockSpec(memory_space=pltpu.SMEM)] + [whole] * len(operands),
        out_specs=whole,
        compiler_params=pltpu.CompilerParams(vmem_limit_bytes=60 * 2**20),
    )(meta, *operands)


def local(size, holders, queries, kv_new, pool, counts, holder_map):
    me = lax.axis_index("request")
    query, new, pool = queries[0], kv_new[0], pool[0]

    def span_of(r):
        return lax.dynamic_index_in_dim(pool, r % holders, 0, keepdims=True)

    own = span_of(me)
    arrived = jnp.concatenate(
        [
            lax.ppermute(span_of(me + s), "request", [(i, (i + s) % holders) for i in range(holders)])
            for s in range(1, holders)
        ],
        axis=0,
    )

    count = lax.dynamic_index_in_dim(counts, me, 0, keepdims=False)
    row = lax.dynamic_index_in_dim(holder_map, me, 0, keepdims=False)
    ranks = jnp.arange(holders, dtype=jnp.int32)
    holder = (me - ranks) % holders
    live = jnp.any((row[:, None] == holder[None, :]) & (ranks[:, None] < count), axis=0)
    meta = jnp.concatenate([lax.axis_index("tensor")[None], live.astype(jnp.int32)])

    new = gather_by_distance(new, size, causal=True)
    near = gather_by_distance(own, size)
    far = gather_by_distance(arrived, size)
    return attend(meta, query, new, list(zip(near, far)))[None]


def solution(mesh):
    placed = (
        P(("group", "request"), "tensor", None),
        P(("group", "request"), "tensor", None),
        P(("group", "request"), None, None, "tensor"),
        P("group"),
        P("group", None),
    )
    return jax.shard_map(
        functools.partial(local, mesh.shape["tensor"], mesh.shape["request"]),
        mesh=mesh,
        in_specs=placed,
        out_specs=P(("group", "request"), "tensor", None),
        check_vma=False,
    )
```

time: 225 us -> 48.1 us (0.21)
  the two profiles are of different devices: /device:TPU:0 before, /device:TPU:11 now
where the time goes in v1:
time: 48.1 us; the launch traced here: 47.9 us
  waiting for transfers between devices  18.8 us (39%)
  starting transfers between devices  13.1 us (27%)
  Pallas kernels  11.5 us (24%)
  local copies, waits for them, and re-layouts  2.91 us (6%)
  other arithmetic  1.34 us (3%)
    pallas_call x1, Pallas kernels, attend(): pl.pallas_call(functools.partial(attend_kernel, size, groups, heads), out...  11.5 us
    ppermute x3, waiting for transfers between devices, local(): lax.ppermute(span_of(me + s), 'request', [(i, (i + s) % holders) for i in...  9.6 us
    ppermute x9, starting transfers between devices, hop(): return lax.ppermute(piece, 'tensor', pairs)  9.24 us
    ppermute x9, waiting for transfers between devices, hop(): return lax.ppermute(piece, 'tensor', pairs)  9.19 us
    ppermute x3, starting transfers between devices, local(): lax.ppermute(span_of(me + s), 'request', [(i, (i + s) % holders) for i in...  3.88 us
    dynamic_slice x1, local copies, waits for them, and re-layouts, span_of(): return lax.dynamic_index_in_dim(pool, r % holders, 0, keepdims=True)  1.19 us
    unnamed x28, local copies, waits for them, and re-layouts  1.12 us
  transfers between devices with their start and end apart: 12, of which 4 were waited for; matrix products, arithmetic and copies ran while one was open for 4% of the time, Pallas kernels for 0%

profile of v1, /device:TPU:11, one launch (start us, length us, event | category | flops | bytes accessed | tf_op | source)
XLA Modules:
  0.0 47.9 jit_solution(17203046244914918235)
XLA Ops:
  0.1 1.2 %dynamic-slice_bitcast_fusion = (bf16[1,128,512]{2,1,0:T(8,128)(2,1)S(1)}, bf16[1,128,512]{2,1,0:T(8,128)(2,1)S(1)}, bf16[1,128,512]{2,1,0:T(8,128)(2,1)S(1)}, bf16[1,128,512]{2,1,0:T(8,128)(2,1)S(1)}) fusion(bf16[1,4,128,512]{3,2,1,0:T(8,128)(2,1)} %param.7, s32[]{:T(128)S(6)} %select_n.57, s32[]{:T(128)S(6)} %select_n.53, s32[]{:T(128)S(6)} %select_n.51, ...), kind=kLoop, calls=%fused_computation | loop fusion | bytes 1048592 | tf_op jit(solution)/shard_map/jit(dynamic_index_in_dim)/dynamic_slice | solution.py:123
  1.3 1.3 %collective-permute-start.3 = (bf16[1,128,512]{2,1,0:T(8,128)(2,1)S(1)}, bf16[1,128,512]{2,1,0:T(8,128)(2,1)S(1)}, u32[]{:S(2)}, u32[]{:S(2)}) collective-permute-start(bf16[1,128,512]{2,1,0:T(8,128)(2,1)S(1)} %get-tuple-element.6), channel_id=1, source_target_pairs={{0,4},{4,8},{8,12},{12,0},{1,5},{5,9},{9,13},{13,1},{2,6},{6,10},{... | collective-permute-start | bytes 393224 | tf_op jit(solution)/shard_map/ppermute | solution.py:128
  2.6 1.1 %collective-permute-start.4 = (bf16[1,128,512]{2,1,0:T(8,128)(2,1)S(1)}, bf16[1,128,512]{2,1,0:T(8,128)(2,1)S(1)}, u32[]{:S(2)}, u32[]{:S(2)}) collective-permute-start(bf16[1,128,512]{2,1,0:T(8,128)(2,1)S(1)} %get-tuple-element.8), channel_id=1, source_target_pairs={{0,8},{4,12},{8,0},{12,4},{1,9},{5,13},{9,1},{13,5},{2,10},{6,14},... | collective-permute-start | bytes 393224 | tf_op jit(solution)/shard_map/ppermute | solution.py:128
  3.7 1.3 %collective-permute-start.1 = (bf16[96,2048]{1,0:T(8,128)(2,1)}, bf16[96,2048]{1,0:T(8,128)(2,1)S(1)}, u32[]{:S(2)}, u32[]{:S(2)}) collective-permute-start(bf16[96,2048]{1,0:T(8,128)(2,1)} %bitcast.16), channel_id=1, source_target_pairs={{0,2},{1,3},{4,6},{5,7},{8,10},{9,11},{12,14},{13,15},{16,18},{17,... | collective-permute-start | bytes 1179656 | tf_op jit(solution)/shard_map/ppermute | solution.py:20
  5.0 1.4 %collective-permute-start.5 = (bf16[1,128,512]{2,1,0:T(8,128)(2,1)S(1)}, bf16[1,128,512]{2,1,0:T(8,128)(2,1)S(1)}, u32[]{:S(2)}, u32[]{:S(2)}) collective-permute-start(bf16[1,128,512]{2,1,0:T(8,128)(2,1)S(1)} %get-tuple-element.5), channel_id=1, source_target_pairs={{0,12},{4,0},{8,4},{12,8},{1,13},{5,1},{9,5},{13,9},{2,14},{6,2},{... | collective-permute-start | bytes 393224 | tf_op jit(solution)/shard_map/ppermute | solution.py:128
  6.4 0.0 collective-permute-done.3
  6.5 6.8 %collective-permute-done.4 = bf16[1,128,512]{2,1,0:T(8,128)(2,1)S(1)} collective-permute-done((bf16[1,128,512]{2,1,0:T(8,128)(2,1)S(1)}, bf16[1,128,512]{2,1,0:T(8,128)(2,1)S(1)}, u32[]{:S(2)}, u32[]{:S(2)}) %collective-permute-start.4) | collective-permute-done | bytes 131104 | tf_op jit(solution)/shard_map/ppermute | solution.py:128
  13.2 2.8 %collective-permute-done.5 = bf16[1,128,512]{2,1,0:T(8,128)(2,1)S(1)} collective-permute-done((bf16[1,128,512]{2,1,0:T(8,128)(2,1)S(1)}, bf16[1,128,512]{2,1,0:T(8,128)(2,1)S(1)}, u32[]{:S(2)}, u32[]{:S(2)}) %collective-permute-start.5) | collective-permute-done | bytes 131104 | tf_op jit(solution)/shard_map/ppermute | solution.py:128
  16.1 0.3 collective-permute-start.9
  16.4 1.2 %collective-permute-start.8 = (bf16[1,128,512]{2,1,0:T(8,128)(2,1)S(1)}, bf16[1,128,512]{2,1,0:T(8,128)(2,1)S(1)}, u32[]{:S(2)}, u32[]{:S(2)}) collective-permute-start(bf16[1,128,512]{2,1,0:T(8,128)(2,1)S(1)} %get-tuple-element.7.refs_5_), channel_id=1, source_target_pairs={{0,2},{1,3},{2,0},{3,1},{4,6},{5,7},{6,4},{7,5},{8,10},{9,11},{10,... | collective-permute-start | bytes 393224 | tf_op jit(solution)/shard_map/ppermute | solution.py:20
  17.6 1.3 %collective-permute-start = (bf16[96,2048]{1,0:T(8,128)(2,1)S(1)}, bf16[96,2048]{1,0:T(8,128)(2,1)S(1)}, u32[]{:S(2)}, u32[]{:S(2)}) collective-permute-start(bf16[96,2048]{1,0:T(8,128)(2,1)S(1)} %bitcast.18), channel_id=1, source_target_pairs={{0,1},{2,3},{4,5},{6,7},{8,9},{10,11},{12,13},{14,15},{16,17},{18,... | collective-permute-start | bytes 1179656 | tf_op jit(solution)/shard_map/ppermute | solution.py:20
  18.9 1.2 %collective-permute-start.6 = (bf16[1,128,512]{2,1,0:T(8,128)(2,1)S(1)}, bf16[1,128,512]{2,1,0:T(8,128)(2,1)S(1)}, u32[]{:S(2)}, u32[]{:S(2)}) collective-permute-start(bf16[1,128,512]{2,1,0:T(8,128)(2,1)S(1)} %get-tuple-element.7.refs_5_), channel_id=1, source_target_pairs={{0,1},{1,0},{2,3},{3,2},{4,5},{5,4},{6,7},{7,6},{8,9},{9,8},{10,11... | collective-permute-start | bytes 393224 | tf_op jit(solution)/shard_map/ppermute | solution.py:20
  20.1 0.6 %dynamic_slice.30 = s32[1]{0:T(128)} dynamic-slice(s32[4]{0:T(128)S(1)} %copy-done.12, s32[]{:T(128)S(6)} %select_n.48), dynamic_slice_sizes={1} | dynamic-slice | bytes 12 | tf_op jit(solution)/shard_map/jit(dynamic_index_in_dim)/dynamic_slice | solution.py:134
  20.7 8.4 %collective-permute-done.8.refs_9_ = bf16[1,128,512]{2,1,0:T(8,128)(2,1)S(1)} collective-permute-done((bf16[1,128,512]{2,1,0:T(8,128)(2,1)S(1)}, bf16[1,128,512]{2,1,0:T(8,128)(2,1)S(1)}, u32[]{:S(2)}, u32[]{:S(2)}) %collective-permute-start.8) | collective-permute-done | bytes 131104 | tf_op jit(solution)/shard_map/ppermute | solution.py:20
  29.2 1.3 %collective-permute-start.7 = (bf16[3,128,512]{2,1,0:T(8,128)(2,1)S(1)}, bf16[3,128,512]{2,1,0:T(8,128)(2,1)S(1)}, u32[]{:S(2)}, u32[]{:S(2)}) collective-permute-start(bf16[3,128,512]{2,1,0:T(8,128)(2,1)S(1)} %constant_dynamic-update-slice_fusion.refs_6_), channel_id=1, source_target_pairs={{0,1},{1,0},{2,3},{3,2},{4,5},{5,4},{6,7},{7,6},{8,9},{9,8},{10,11... | collective-permute-start | bytes 1179656 | tf_op jit(solution)/shard_map/ppermute | solution.py:20
  30.5 1.9 %collective-permute-start.2 = (bf16[96,2048]{1,0:T(8,128)(2,1)S(1)}, bf16[96,2048]{1,0:T(8,128)(2,1)S(1)}, u32[]{:S(2)}, u32[]{:S(2)}) collective-permute-start(bf16[96,2048]{1,0:T(8,128)(2,1)S(1)} %collective-permute-done.1.refs_3_), channel_id=1, source_target_pairs={{2,3},{3,2},{6,7},{7,6},{10,11},{11,10},{14,15},{15,14},{18,19},{1... | collective-permute-start | bytes 1179656 | tf_op jit(solution)/shard_map/ppermute | solution.py:20
  32.4 0.0 collective-permute-done.9.refs_10_
  32.4 0.6 %collective-permute-start.11 = (bf16[3,128,512]{2,1,0:T(8,128)(2,1)S(1)}, bf16[3,128,512]{2,1,0:T(8,128)(2,1)S(1)}, u32[]{:S(2)}, u32[]{:S(2)}) collective-permute-start(bf16[3,128,512]{2,1,0:T(8,128)(2,1)S(1)} %collective-permute-done.9.refs_10_), channel_id=1, source_target_pairs={{0,1},{1,0},{2,3},{3,2},{4,5},{5,4},{6,7},{7,6},{8,9},{9,8},{10,11... | collective-permute-start | bytes 1179656 | tf_op jit(solution)/shard_map/ppermute | solution.py:20
  33.0 0.6 %iota_compare_fusion = pred[4]{0:T(512)(128)(4,1)S(1)} fusion(s32[]{:T(128)} %bitcast.2), kind=kLoop, calls=%fused_computation.15 | loop fusion | flops 4 | bytes 8 | tf_op jit(solution)/shard_map/lt | solution.py:138
  33.7 0.1 collective-permute-start.10
  33.8 0.1 and_reduce_fusion
  33.9 0.6 %pad_add_fusion.meta = s32[5]{0:T(128)} fusion(s32[4]{0:T(128)S(1)} %convert_element_type.3, s32[1]{0:T(128)} %bitcast), kind=kLoop, calls=%fused_computation.14 | loop fusion | flops 5 | bytes 40 | tf_op jit(solution)/shard_map/concatenate | solution.py:139
  34.5 0.7 %collective-permute-done.10.refs_11_ = bf16[1,128,512]{2,1,0:T(8,128)(2,1)} collective-permute-done((bf16[1,128,512]{2,1,0:T(8,128)(2,1)S(1)}, bf16[1,128,512]{2,1,0:T(8,128)(2,1)}, u32[]{:S(2)}, u32[]{:S(2)}) %collective-permute-start.10) | collective-permute-done | bytes 131104 | tf_op jit(solution)/shard_map/ppermute | solution.py:20
  35.2 0.0 collective-permute-done.refs_2_
  35.3 0.0 collective-permute-done.7.refs_8_
  35.3 0.0 collective-permute-done.2.refs_4_
  35.3 0.0 collective-permute-done.11.refs_12_
  35.4 0.6 %copy-done.6 = bf16[96,2048]{1,0:T(8,128)(2,1)} copy-done((bf16[96,2048]{1,0:T(8,128)(2,1)}, bf16[96,2048]{1,0:T(8,128)(2,1)S(1)}, u32[]{:S(2)}) %copy-start.6) | copy-done | bytes 393240
  36.0 0.1 copy-done.7
  36.1 0.2 copy-done.8
  36.3 0.1 copy-done.9
  36.4 11.5 %shard_map.55 = bf16[96,8192]{1,0:T(8,128)(2,1)} custom-call(s32[5]{0:T(128)} %pad_add_fusion.meta, bf16[96,8192]{1,0:T(8,128)(2,1)} %bitcast.15, bf16[96,2048]{1,0:T(8,128)(2,1)} %bitcast.17, bf16[96,2048]{1,0:T(8,128)(2,1)} %copy-done.6, bf16[96,2048]{1,0:T(8,128)(2,1)} %copy-done.4, bf16[96,2048]{1,0:T(8,128)(2,1)} %copy-done.8, ...), custom_call_target="tpu_custom_call" | custom-call | tf_op jit(solution)/shard_map/pallas_call | solution.py:109
  (30 shorter events, 0.1 us)
Async XLA Ops:
  0.0 33.7 %copy-start = (s32[4,4]{1,0:T(4,128)S(1)}, s32[4,4]{1,0:T(4,128)}, u32[]{:S(2)}) copy-start(s32[4,4]{1,0:T(4,128)} %param.9) | copy-start | bytes 196
  0.0 17.6 %copy-start.3 = (bf16[1,96,2048]{2,1,0:T(8,128)(2,1)S(1)}, bf16[1,96,2048]{2,1,0:T(8,128)(2,1)}, u32[]{:S(2)}) copy-start(bf16[1,96,2048]{2,1,0:T(8,128)(2,1)} %param.6) | copy-start | bytes 1179652
  0.0 20.1 %copy-start.12 = (s32[4]{0:T(128)S(1)}, s32[4]{0:T(128)}, u32[]{:S(2)}) copy-start(s32[4]{0:T(128)} %param.8) | copy-start | bytes 52
  1.3 34.1 %copy-start.2 = (bf16[1,128,512]{2,1,0:T(8,128)(2,1)}, bf16[1,128,512]{2,1,0:T(8,128)(2,1)S(1)}, u32[]{:S(2)}) copy-start(bf16[1,128,512]{2,1,0:T(8,128)(2,1)S(1)} %get-tuple-element.7.refs_5_) | copy-start | bytes 393220
  1.3 5.2 %collective-permute-start.3 = (bf16[1,128,512]{2,1,0:T(8,128)(2,1)S(1)}, bf16[1,128,512]{2,1,0:T(8,128)(2,1)S(1)}, u32[]{:S(2)}, u32[]{:S(2)}) collective-permute-start(bf16[1,128,512]{2,1,0:T(8,128)(2,1)S(1)} %get-tuple-element.6), channel_id=1, source_target_pairs={{0,4},{4,8},{8,12},{12,0},{1,5},{5,9},{9,13},{13,1},{2,6},{6,10},{... | collective-permute-start | bytes 393224 | tf_op jit(solution)/shard_map/ppermute | solution.py:128
  2.6 10.6 %collective-permute-start.4 = (bf16[1,128,512]{2,1,0:T(8,128)(2,1)S(1)}, bf16[1,128,512]{2,1,0:T(8,128)(2,1)S(1)}, u32[]{:S(2)}, u32[]{:S(2)}) collective-permute-start(bf16[1,128,512]{2,1,0:T(8,128)(2,1)S(1)} %get-tuple-element.8), channel_id=1, source_target_pairs={{0,8},{4,12},{8,0},{12,4},{1,9},{5,13},{9,1},{13,5},{2,10},{6,14},... | collective-permute-start | bytes 393224 | tf_op jit(solution)/shard_map/ppermute | solution.py:128
  3.7 26.8 %collective-permute-start.1 = (bf16[96,2048]{1,0:T(8,128)(2,1)}, bf16[96,2048]{1,0:T(8,128)(2,1)S(1)}, u32[]{:S(2)}, u32[]{:S(2)}) collective-permute-start(bf16[96,2048]{1,0:T(8,128)(2,1)} %bitcast.16), channel_id=1, source_target_pairs={{0,2},{1,3},{4,6},{5,7},{8,10},{9,11},{12,14},{13,15},{16,18},{17,... | collective-permute-start | bytes 1179656 | tf_op jit(solution)/shard_map/ppermute | solution.py:20
  5.0 11.1 %collective-permute-start.5 = (bf16[1,128,512]{2,1,0:T(8,128)(2,1)S(1)}, bf16[1,128,512]{2,1,0:T(8,128)(2,1)S(1)}, u32[]{:S(2)}, u32[]{:S(2)}) collective-permute-start(bf16[1,128,512]{2,1,0:T(8,128)(2,1)S(1)} %get-tuple-element.5), channel_id=1, source_target_pairs={{0,12},{4,0},{8,4},{12,8},{1,13},{5,1},{9,5},{13,9},{2,14},{6,2},{... | collective-permute-start | bytes 393224 | tf_op jit(solution)/shard_map/ppermute | solution.py:128
  16.1 19.2 %copy-start.1 = (bf16[3,128,512]{2,1,0:T(8,128)(2,1)}, bf16[3,128,512]{2,1,0:T(8,128)(2,1)S(1)}, u32[]{:S(2)}) copy-start(bf16[3,128,512]{2,1,0:T(8,128)(2,1)S(1)} %constant_dynamic-update-slice_fusion.refs_6_) | copy-start | bytes 1179652
  16.1 16.3 %collective-permute-start.9 = (bf16[3,128,512]{2,1,0:T(8,128)(2,1)S(1)}, bf16[3,128,512]{2,1,0:T(8,128)(2,1)S(1)}, u32[]{:S(2)}, u32[]{:S(2)}) collective-permute-start(bf16[3,128,512]{2,1,0:T(8,128)(2,1)S(1)} %constant_dynamic-update-slice_fusion.refs_6_), channel_id=1, source_target_pairs={{0,2},{1,3},{2,0},{3,1},{4,6},{5,7},{6,4},{7,5},{8,10},{9,11},{10,... | collective-permute-start | bytes 1179656 | tf_op jit(solution)/shard_map/ppermute | solution.py:20
  16.4 12.7 %collective-permute-start.8 = (bf16[1,128,512]{2,1,0:T(8,128)(2,1)S(1)}, bf16[1,128,512]{2,1,0:T(8,128)(2,1)S(1)}, u32[]{:S(2)}, u32[]{:S(2)}) collective-permute-start(bf16[1,128,512]{2,1,0:T(8,128)(2,1)S(1)} %get-tuple-element.7.refs_5_), channel_id=1, source_target_pairs={{0,2},{1,3},{2,0},{3,1},{4,6},{5,7},{6,4},{7,5},{8,10},{9,11},{10,... | collective-permute-start | bytes 393224 | tf_op jit(solution)/shard_map/ppermute | solution.py:20
  17.6 17.6 %collective-permute-start = (bf16[96,2048]{1,0:T(8,128)(2,1)S(1)}, bf16[96,2048]{1,0:T(8,128)(2,1)S(1)}, u32[]{:S(2)}, u32[]{:S(2)}) collective-permute-start(bf16[96,2048]{1,0:T(8,128)(2,1)S(1)} %bitcast.18), channel_id=1, source_target_pairs={{0,1},{2,3},{4,5},{6,7},{8,9},{10,11},{12,13},{14,15},{16,17},{18,... | collective-permute-start | bytes 1179656 | tf_op jit(solution)/shard_map/ppermute | solution.py:20
  18.9 14.8 %collective-permute-start.6 = (bf16[1,128,512]{2,1,0:T(8,128)(2,1)S(1)}, bf16[1,128,512]{2,1,0:T(8,128)(2,1)S(1)}, u32[]{:S(2)}, u32[]{:S(2)}) collective-permute-start(bf16[1,128,512]{2,1,0:T(8,128)(2,1)S(1)} %get-tuple-element.7.refs_5_), channel_id=1, source_target_pairs={{0,1},{1,0},{2,3},{3,2},{4,5},{5,4},{6,7},{7,6},{8,9},{9,8},{10,11... | collective-permute-start | bytes 393224 | tf_op jit(solution)/shard_map/ppermute | solution.py:20
  29.2 6.2 %copy-start.10 = (bf16[1,128,512]{2,1,0:T(8,128)(2,1)}, bf16[1,128,512]{2,1,0:T(8,128)(2,1)S(1)}, u32[]{:S(2)}) copy-start(bf16[1,128,512]{2,1,0:T(8,128)(2,1)S(1)} %collective-permute-done.8.refs_9_) | copy-start | bytes 393220
  29.2 6.1 %collective-permute-start.7 = (bf16[3,128,512]{2,1,0:T(8,128)(2,1)S(1)}, bf16[3,128,512]{2,1,0:T(8,128)(2,1)S(1)}, u32[]{:S(2)}, u32[]{:S(2)}) collective-permute-start(bf16[3,128,512]{2,1,0:T(8,128)(2,1)S(1)} %constant_dynamic-update-slice_fusion.refs_6_), channel_id=1, source_target_pairs={{0,1},{1,0},{2,3},{3,2},{4,5},{5,4},{6,7},{7,6},{8,9},{9,8},{10,11... | collective-permute-start | bytes 1179656 | tf_op jit(solution)/shard_map/ppermute | solution.py:20
  30.5 4.8 %copy-start.4 = (bf16[96,2048]{1,0:T(8,128)(2,1)}, bf16[96,2048]{1,0:T(8,128)(2,1)S(1)}, u32[]{:S(2)}) copy-start(bf16[96,2048]{1,0:T(8,128)(2,1)S(1)} %collective-permute-done.1.refs_3_) | copy-start | bytes 1179652
  30.5 4.8 %collective-permute-start.2 = (bf16[96,2048]{1,0:T(8,128)(2,1)S(1)}, bf16[96,2048]{1,0:T(8,128)(2,1)S(1)}, u32[]{:S(2)}, u32[]{:S(2)}) collective-permute-start(bf16[96,2048]{1,0:T(8,128)(2,1)S(1)} %collective-permute-done.1.refs_3_), channel_id=1, source_target_pairs={{2,3},{3,2},{6,7},{7,6},{10,11},{11,10},{14,15},{15,14},{18,19},{1... | collective-permute-start | bytes 1179656 | tf_op jit(solution)/shard_map/ppermute | solution.py:20
  32.4 2.9 %copy-start.5 = (bf16[3,128,512]{2,1,0:T(8,128)(2,1)}, bf16[3,128,512]{2,1,0:T(8,128)(2,1)S(1)}, u32[]{:S(2)}) copy-start(bf16[3,128,512]{2,1,0:T(8,128)(2,1)S(1)} %collective-permute-done.9.refs_10_) | copy-start | bytes 1179652
  32.4 2.8 %collective-permute-start.11 = (bf16[3,128,512]{2,1,0:T(8,128)(2,1)S(1)}, bf16[3,128,512]{2,1,0:T(8,128)(2,1)S(1)}, u32[]{:S(2)}, u32[]{:S(2)}) collective-permute-start(bf16[3,128,512]{2,1,0:T(8,128)(2,1)S(1)} %collective-permute-done.9.refs_10_), channel_id=1, source_target_pairs={{0,1},{1,0},{2,3},{3,2},{4,5},{5,4},{6,7},{7,6},{8,9},{9,8},{10,11... | collective-permute-start | bytes 1179656 | tf_op jit(solution)/shard_map/ppermute | solution.py:20
  33.7 1.7 %copy-start.11 = (bf16[1,128,512]{2,1,0:T(8,128)(2,1)}, bf16[1,128,512]{2,1,0:T(8,128)(2,1)S(1)}, u32[]{:S(2)}) copy-start(bf16[1,128,512]{2,1,0:T(8,128)(2,1)S(1)} %collective-permute-done.6.refs_7_) | copy-start | bytes 393220
  33.7 1.5 %collective-permute-start.10 = (bf16[1,128,512]{2,1,0:T(8,128)(2,1)S(1)}, bf16[1,128,512]{2,1,0:T(8,128)(2,1)}, u32[]{:S(2)}, u32[]{:S(2)}) collective-permute-start(bf16[1,128,512]{2,1,0:T(8,128)(2,1)S(1)} %collective-permute-done.8.refs_9_), channel_id=1, source_target_pairs={{0,1},{1,0},{2,3},{3,2},{4,5},{5,4},{6,7},{7,6},{8,9},{9,8},{10,11... | collective-permute-start | bytes 393224 | tf_op jit(solution)/shard_map/ppermute | solution.py:20
  35.3 0.7 %copy-start.6 = (bf16[96,2048]{1,0:T(8,128)(2,1)}, bf16[96,2048]{1,0:T(8,128)(2,1)S(1)}, u32[]{:S(2)}) copy-start(bf16[96,2048]{1,0:T(8,128)(2,1)S(1)} %collective-permute-done.refs_2_) | copy-start | bytes 1179652
  35.3 0.9 %copy-start.7 = (bf16[3,128,512]{2,1,0:T(8,128)(2,1)}, bf16[3,128,512]{2,1,0:T(8,128)(2,1)S(1)}, u32[]{:S(2)}) copy-start(bf16[3,128,512]{2,1,0:T(8,128)(2,1)S(1)} %collective-permute-done.7.refs_8_) | copy-start | bytes 1179652
  35.3 1.0 %copy-start.8 = (bf16[96,2048]{1,0:T(8,128)(2,1)}, bf16[96,2048]{1,0:T(8,128)(2,1)S(1)}, u32[]{:S(2)}) copy-start(bf16[96,2048]{1,0:T(8,128)(2,1)S(1)} %collective-permute-done.2.refs_4_) | copy-start | bytes 1179652
  35.3 1.1 %copy-start.9 = (bf16[3,128,512]{2,1,0:T(8,128)(2,1)}, bf16[3,128,512]{2,1,0:T(8,128)(2,1)S(1)}, u32[]{:S(2)}) copy-start(bf16[3,128,512]{2,1,0:T(8,128)(2,1)S(1)} %collective-permute-done.11.refs_12_) | copy-start | bytes 1179652

commit v2 on v0

v2 whole, which is shorter than its diff:
```python
import functools
import math
import typing

import jax
import jax.numpy as jnp
from jax import lax
from jax.experimental import pallas as pl
from jax.experimental.pallas import tpu as pltpu
from jax.sharding import PartitionSpec as P

HD = 128
NEG = -math.inf
CHUNK = 96 * 256
TO_EXP2 = HD**-0.5 * math.log2(math.e)
VMEM = pl.BlockSpec(memory_space=pltpu.VMEM)
SMEM = pl.BlockSpec(memory_space=pltpu.SMEM)
HBM = pl.BlockSpec(memory_space=pltpu.HBM)


def attend_kernel(size, jobs, pieces, states, counts, holder_map, *refs):
    resumed, chained, left, ended = states
    refs = list(refs)

    def take(n):
        return [refs.pop(0) for _ in range(n)]

    (q_ref,) = take(1)
    new = take(size if any(job.fresh for job in jobs) else 0)
    far = dict(zip(pieces, take(len(pieces))))
    peak_in, sums_in = take(2) if resumed else (None, None)
    take(chained)
    peak_out, sums_out = take(2) if left else (None, None)
    o_ref, done, sem = take(3) if ended else (None, None, None)

    me, request = lax.axis_index("tensor"), lax.axis_index("request")
    holders = holder_map.shape[1]
    tokens = q_ref.shape[0]
    local_kv = max(job.head for job in jobs) + 1
    heads = q_ref.shape[1] // HD // (size * local_kv)
    rows = heads * tokens

    def bias_of(job):
        fresh = size * tokens if job.fresh else 0
        sizes = [(first, *far[first, job.distance].shape[:2]) for first in job.far]
        keys = fresh + sum(count * span for _, count, span in sizes)
        column = lax.broadcasted_iota(jnp.int32, (1, keys), 1)
        bias = jnp.zeros((1, keys), jnp.float32)
        if job.fresh:
            for d in range(1, size):
                hidden = jnp.bitwise_xor(me, d) > me
                here = (column >= tokens * d) & (column < tokens * (d + 1))
                bias = jnp.where(here & hidden, NEG, bias)
        start = fresh
        for first, count, span in sizes:
            for c in range(holders):
                place = lax.rem(request - holder_map[request, c] + holders, holders) - first
                at = start + place * span
                here = (column >= at) & (column < at + span)
                here &= (place >= 0) & (place < count) & (c >= counts[request])
                bias = jnp.where(here, NEG, bias)
            start += count * span
        return bias

    lead = -(-tokens // HD) * HD

    def with_causal(bias):
        row = lax.broadcasted_iota(jnp.int32, (tokens, lead), 0)
        col = lax.broadcasted_iota(jnp.int32, (tokens, lead), 1)
        return jnp.where((row < col) & (col < tokens), NEG, bias[:, :lead])

    def kind(job):
        return job.fresh, *((first, far[first, job.distance].shape[0]) for first in job.far)

    biases = {}
    for job in jobs:
        if kind(job) not in biases:
            bias = bias_of(job)
            biases[kind(job)] = bias, with_causal(bias) if job.fresh else None

    def side(job, which):
        blocks = []
        if job.fresh:
            head = jnp.bitwise_xor(me, job.distance) * local_kv + job.head
            at = pl.ds(pl.multiple_of((2 * head + which) * HD, HD), HD)
            blocks += [ref[:, at] for ref in new]
        at = slice((2 * job.head + which) * HD, (2 * job.head + which + 1) * HD)
        for first in job.far:
            piece = far[first, job.distance]
            blocks += [piece[s, :, at] for s in range(piece.shape[0])]
        return jnp.concatenate(blocks, axis=0)

    def columns(job, h=0, count=1):
        head = (jnp.bitwise_xor(me, job.distance) * local_kv + job.head) * heads + h
        return pl.ds(pl.multiple_of(head * HD, HD), count * HD)

    def scores_of(job):
        query = jnp.concatenate([q_ref[:, columns(job, h)] for h in range(heads)], axis=0)
        return lax.dot_general(
            query, side(job, 0), (((1,), (1,)), ((), ())), preferred_element_type=jnp.float32
        )

    copies = []

    def finish(job, scores):
        bias, causal = biases[kind(job)]
        keys = bias.shape[1]
        fit = [n for n in range(16, tokens + 1, 16) if tokens % n == 0 and n * keys <= CHUNK]
        chunk = max(fit, default=16)
        weights, scales = [], []
        for at in range(0, rows, chunk):
            here = slice(at, at + chunk)
            part = scores[here]
            if job.fresh:
                row = at % tokens
                part = jnp.concatenate(
                    [part[:, :lead] + causal[row : row + chunk], part[:, lead:] + bias[:, lead:]],
                    axis=1,
                )
            else:
                part = part + bias
            peak = jnp.broadcast_to(jnp.max(part, axis=1, keepdims=True), (chunk, HD))
            if job.resume is not None:
                before = peak_in[job.resume, here]
                peak = jnp.maximum(peak, before)
                scales.append(jnp.exp2((before - peak) * TO_EXP2))
            if job.leave is not None:
                peak_out[job.leave, here] = peak
            part = part - jnp.concatenate([peak] * (keys // HD), axis=1)
            weights.append(jnp.exp2(part * TO_EXP2).astype(jnp.bfloat16))
        value = side(job, 1)
        value = jnp.concatenate([value, jnp.ones_like(value)], axis=1)
        all_sums = jnp.dot(
            jnp.concatenate(weights, axis=0), value, preferred_element_type=jnp.float32
        )
        slot = len(copies)
        for n, at in enumerate(range(0, rows, chunk)):
            here = slice(at, at + chunk)
            sums = all_sums[here]
            if job.resume is not None:
                sums = sums + sums_in[job.resume, here] * jnp.concatenate([scales[n]] * 2, axis=1)
            if job.leave is not None:
                sums_out[job.leave, here] = sums
            else:
                h, row = at // tokens * HD, at % tokens
                out = (sums[:, :HD] / sums[:, HD:]).astype(o_ref.dtype)
                done[slot, row : row + chunk, h : h + HD] = out
        if job.leave is None:
            copy = pltpu.make_async_copy(
                done.at[slot], o_ref.at[:, columns(job, 0, heads)], sem.at[slot]
            )
            copy.start()
            copies.append(copy)

    scores = scores_of(jobs[0])
    for n, job in enumerate(jobs):
        later = scores_of(jobs[n + 1]) if n + 1 < len(jobs) else None
        finish(job, scores)
        scores = later
    for copy in copies:
        copy.wait()


class Job(typing.NamedTuple):
    distance: int
    head: int
    fresh: bool
    far: tuple
    resume: int | None
    leave: int | None


def attend(rules, query, new, far, jobs, state=None, out=None):
    pieces = tuple(far)
    tokens, columns = query.shape
    _, span, width = far[pieces[0]].shape if far else (0, 0, new[0].shape[1] // len(new))
    local_kv = width // (2 * HD)
    size = new[0].shape[1] // width
    heads = columns // HD // (size * local_kv)
    rows = heads * tokens
    left = sum(job.leave is not None for job in jobs)
    ended = len(jobs) - left
    fresh = any(job.fresh for job in jobs)
    operands = [query, *(new if fresh else ()), *far.values(), *(state or ())]
    chained = [out] if out is not None else []
    keys = [
        size * tokens * job.fresh + sum(far[first, job.distance].shape[0] * span for first in job.far)
        for job in jobs
    ]
    shapes, specs, scratch = [], [], []
    if left:
        shapes += [
            jax.ShapeDtypeStruct((left, rows, HD), jnp.float32),
            jax.ShapeDtypeStruct((left, rows, 2 * HD), jnp.float32),
        ]
        specs += [VMEM, VMEM]
    if ended:
        shapes += [jax.ShapeDtypeStruct(query.shape, query.dtype)]
        specs += [HBM]
        scratch = [
            pltpu.VMEM((ended, tokens, heads * HD), query.dtype),
            pltpu.SemaphoreType.DMA((ended,)),
        ]
    states = (state is not None, len(chained), left, ended)
    results = pl.pallas_call(
        functools.partial(attend_kernel, size, jobs, pieces, states),
        out_shape=shapes,
        in_specs=[SMEM, SMEM] + [VMEM] * len(operands) + [HBM] * len(chained),
        out_specs=specs,
        scratch_shapes=scratch,
        input_output_aliases={2 + len(operands): len(shapes) - 1} if chained else {},
        cost_estimate=pl.CostEstimate(
            flops=8 * HD * rows * sum(keys), bytes_accessed=0, transcendentals=rows * sum(keys)
        ),
        compiler_params=pltpu.CompilerParams(
            vmem_limit_bytes=16 * rows * max(keys) + 10 * 2**20
        ),
    )(*rules, *operands, *chained)
    return (results[:2] if left else None), (results[-1] if ended else None)


def local(size, holders, queries, kv_new, pool, counts, holder_map):
    query, new, pool = queries[0], kv_new[0], pool[0]
    request = lax.axis_index("request")
    rules = (counts, holder_map)
    half = size // 2
    inner = [half >> (n + 1) for n in range(half.bit_length() - 1)]

    def swap(piece, bit):
        return lax.ppermute(piece, "tensor", [(i, i ^ bit) for i in range(size)])

    def spread(piece, bits):
        held = {0: piece}
        for bit in bits:
            for distance in sorted(held):
                held[distance + bit] = swap(held[distance], bit)
        return [held[d] for d in sorted(held)]

    def after(piece, others):
        return lax.optimization_barrier((piece, others))[0]

    def span_of(r):
        return lax.dynamic_index_in_dim(pool, lax.rem(r, holders), 0, keepdims=True)

    new_away = swap(new, half)
    spans = [span_of(request)]
    for s in range(1, holders):
        pairs = [(i, (i + s) % holders) for i in range(holders)]
        spans.append(lax.ppermute(span_of(request + s), "request", pairs))
    early = jnp.concatenate(spans[:2], axis=0)
    early_away = swap(early, half)

    new = spread(new, inner) + spread(new_away, inner)
    local_kv = pool.shape[2] // (2 * HD)
    order = [(d, i) for d in range(size) for i in range(local_kv)]
    home, away = order[: len(order) // 2], order[len(order) // 2 :]

    late_away = swap(jnp.concatenate(spans[2:], axis=0), half)

    far = {(0, d): piece for d, piece in enumerate(spread(jnp.concatenate(spans, axis=0), inner))}
    far |= {(0, half + d): piece for d, piece in enumerate(spread(early_away, inner))}
    jobs = [Job(d, i, True, (0,), None, None) for d, i in home]
    jobs += [Job(d, i, True, (0,), None, n) for n, (d, i) in enumerate(away)]
    state, out = attend(rules, query, new, far, jobs)

    late_away = after(late_away, state)
    far = {(2, half + d): piece for d, piece in enumerate(spread(late_away, inner))}
    jobs = [Job(d, i, False, (2,), n, None) for n, (d, i) in enumerate(away)]
    return attend(rules, query, new, far, jobs, state, out)[1][None]


def solution(mesh):
    placed = (
        P(("group", "request"), "tensor", None),
        P(("group", "request"), "tensor", None),
        P(("group", "request"), None, None, "tensor"),
        P("group"),
        P("group", None),
    )
    return jax.shard_map(
        functools.partial(local, mesh.shape["tensor"], mesh.shape["request"]),
        mesh=mesh,
        in_specs=placed,
        out_specs=P(("group", "request"), "tensor", None),
        check_vma=False,
    )
```

time: 225 us -> 34.7 us (0.15)
  other arithmetic: 79.2 us -> 0.12 us
  local copies, waits for them, and re-layouts: 64 us -> 1.29 us
  blocking collectives: 23.3 us -> 0 us
  waiting for transfers between devices: 27.6 us -> 9.95 us
  matrix products: 15 us -> 0 us
  Pallas kernels: 0 us -> 10.5 us
    unnamed x3 -> x0, other arithmetic: 67.8 us -> none
    unnamed x28 -> x8, local copies, waits for them, and re-layouts: 33.1 us -> 0.01 us
    all_to_all x3 -> x0, waiting for transfers between devices: 27.6 us -> none  [the longest x1 17.3 us: local(): lax.all_to_all(queries, 'tensor', split_axis=2, concat_axis=1, tiled=True)]
    all_to_all x1 -> x0, blocking collectives: 23.3 us -> none  [local(): lax.all_to_all(result, 'tensor', split_axis=1, concat_axis=2, tiled=True)]
    dot_general x32 -> x0, matrix products: 15 us -> none  [the longest x16 7.51 us: attend_joint(): jnp.dot(weights.astype(jnp.bfloat16), values_all, preferred_element_type=...]
    all_to_all x7 -> x0, local copies, waits for them, and re-layouts: 15 us -> none  [the longest x3 12.8 us: local(): lax.all_to_all(queries, 'tensor', split_axis=2, concat_axis=1, tiled=True)]
    all_to_all x3 -> x0, starting transfers between devices: 13.8 us -> none  [the longest x1 5.79 us: local(): lax.all_to_all(pool, 'request', split_axis=1, concat_axis=0, tiled=True)]
    ppermute x0 -> x11, starting transfers between devices: none -> 12.6 us  [the longest x8 6.47 us: swap(): return lax.ppermute(piece, 'tensor', [(i, i ^ bit) for i in range(size)])]
  transfers between devices with their start and end apart: 3 -> 11, of which waited for: 2 -> 5; matrix products, arithmetic and copies ran while one was open for 30% -> 0% of each run, Pallas kernels for 0% -> 22%
where the time goes in v2:
time: 34.7 us; the launch traced here: 34.5 us
  starting transfers between devices  12.6 us (36%)
  Pallas kernels  10.5 us (30%)
  waiting for transfers between devices  9.95 us (29%)
  local copies, waits for them, and re-layouts  1.29 us (4%)
    pallas_call x2, Pallas kernels, attend(): pl.pallas_call(functools.partial(attend_kernel, size, jobs, pieces, state...  10.5 us
    ppermute x3, waiting for transfers between devices, local(): spans.append(lax.ppermute(span_of(request + s), 'request', pairs))  6.91 us
    ppermute x8, starting transfers between devices, swap(): return lax.ppermute(piece, 'tensor', [(i, i ^ bit) for i in range(size)])  6.47 us
    ppermute x3, starting transfers between devices, local(): spans.append(lax.ppermute(span_of(request + s), 'request', pairs))  6.13 us
    ppermute x8, waiting for transfers between devices, swap(): return lax.ppermute(piece, 'tensor', [(i, i ^ bit) for i in range(size)])  3.04 us
    dynamic_slice x1, local copies, waits for them, and re-layouts, span_of(): return lax.dynamic_index_in_dim(pool, lax.rem(r, holders), 0, keepdims=True)  1.27 us
  transfers between devices with their start and end apart: 11, of which 5 were waited for; matrix products, arithmetic and copies ran while one was open for 0% of the time, Pallas kernels for 22%

profile of v2, /device:TPU:0, one launch (start us, length us, event | category | flops | bytes accessed | tf_op | source)
XLA Modules:
  0.0 34.5 jit_solution(553402192713912896)
XLA Ops:
  0.0 0.0 copy-start.3
  0.0 0.0 copy-start
  0.0 1.3 %dynamic-slice_bitcast_fusion.1 = (bf16[1,128,512]{2,1,0:T(8,128)(2,1)S(1)}, bf16[1,128,512]{2,1,0:T(8,128)(2,1)S(1)}, bf16[1,128,512]{2,1,0:T(8,128)(2,1)S(1)}, bf16[1,128,512]{2,1,0:T(8,128)(2,1)S(1)}) fusion(bf16[1,4,128,512]{3,2,1,0:T(8,128)(2,1)} %param.7, s32[]{:T(128)S(6)} %select_n.15, s32[]{:T(128)S(6)} %select_n.14, s32[]{:T(128)S(6)} %select_n.13, ...), kind=kLoop, calls=%fused_computation.4 | loop fusion | bytes 1048592 | tf_op jit(solution)/shard_map/jit(dynamic_index_in_dim)/dynamic_slice | solution.py:243
  1.3 3.1 %collective-permute-start.6 = (bf16[1,128,512]{2,1,0:T(8,128)(2,1)S(1)}, bf16[1,128,512]{2,1,0:T(8,128)(2,1)S(1)}, u32[]{:S(2)}, u32[]{:S(2)}) collective-permute-start(bf16[1,128,512]{2,1,0:T(8,128)(2,1)S(1)} %get-tuple-element.16), channel_id=1, source_target_pairs={{0,4},{4,8},{8,12},{12,0},{1,5},{5,9},{9,13},{13,1},{2,6},{6,10},{... | collective-permute-start | bytes 393224 | tf_op jit(solution)/shard_map/ppermute | solution.py:249
  4.4 1.5 %collective-permute-start.4 = (bf16[96,2048]{1,0:T(8,128)(2,1)}, bf16[96,2048]{1,0:T(8,128)(2,1)S(1)}, u32[]{:S(2)}, u32[]{:S(2)}) collective-permute-start(bf16[96,2048]{1,0:T(8,128)(2,1)} %bitcast.13), channel_id=1, source_target_pairs={{0,2},{1,3},{2,0},{3,1},{4,6},{5,7},{6,4},{7,5},{8,10},{9,11},{10,... | collective-permute-start | bytes 1179656 | tf_op jit(solution)/shard_map/ppermute | solution.py:230
  5.9 2.2 %collective-permute-start.1 = (bf16[1,128,512]{2,1,0:T(8,128)(2,1)S(1)}, bf16[1,128,512]{2,1,0:T(8,128)(2,1)S(1)}, u32[]{:S(2)}, u32[]{:S(2)}) collective-permute-start(bf16[1,128,512]{2,1,0:T(8,128)(2,1)S(1)} %get-tuple-element.14), channel_id=1, source_target_pairs={{0,12},{4,0},{8,4},{12,8},{1,13},{5,1},{9,5},{13,9},{2,14},{6,2},{... | collective-permute-start | bytes 393224 | tf_op jit(solution)/shard_map/ppermute | solution.py:249
  8.1 0.8 %collective-permute-start = (bf16[1,128,512]{2,1,0:T(8,128)(2,1)S(1)}, bf16[1,128,512]{2,1,0:T(8,128)(2,1)S(1)}, u32[]{:S(2)}, u32[]{:S(2)}) collective-permute-start(bf16[1,128,512]{2,1,0:T(8,128)(2,1)S(1)} %get-tuple-element.15), channel_id=1, source_target_pairs={{0,8},{4,12},{8,0},{12,4},{1,9},{5,13},{9,1},{13,5},{2,10},{6,14},... | collective-permute-start | bytes 393224 | tf_op jit(solution)/shard_map/ppermute | solution.py:249
  8.9 1.1 %collective-permute-done.6 = bf16[1,128,512]{2,1,0:T(8,128)(2,1)S(1)} collective-permute-done((bf16[1,128,512]{2,1,0:T(8,128)(2,1)S(1)}, bf16[1,128,512]{2,1,0:T(8,128)(2,1)S(1)}, u32[]{:S(2)}, u32[]{:S(2)}) %collective-permute-start.6) | collective-permute-done | bytes 131104 | tf_op jit(solution)/shard_map/ppermute | solution.py:249
  10.1 2.5 %collective-permute-start.8 = (bf16[2,128,512]{2,1,0:T(8,128)(2,1)S(1)}, bf16[2,128,512]{2,1,0:T(8,128)(2,1)S(1)}, u32[]{:S(2)}, u32[]{:S(2)}) collective-permute-start(bf16[2,128,512]{2,1,0:T(8,128)(2,1)S(1)} %pad_maximum_fusion.2), channel_id=1, source_target_pairs={{0,2},{1,3},{2,0},{3,1},{4,6},{5,7},{6,4},{7,5},{8,10},{9,11},{10,... | collective-permute-start | bytes 786440 | tf_op jit(solution)/shard_map/ppermute | solution.py:230
  12.6 0.1 collective-permute-done.1
  12.7 5.6 %collective-permute-done = bf16[1,128,512]{2,1,0:T(8,128)(2,1)S(1)} collective-permute-done((bf16[1,128,512]{2,1,0:T(8,128)(2,1)S(1)}, bf16[1,128,512]{2,1,0:T(8,128)(2,1)S(1)}, u32[]{:S(2)}, u32[]{:S(2)}) %collective-permute-start) | collective-permute-done | bytes 131104 | tf_op jit(solution)/shard_map/ppermute | solution.py:249
  18.3 0.1 pad_maximum_fusion.refs_5_
  18.4 0.1 collective-permute-start.7
  18.5 0.0 copy-done.3
  18.5 0.5 %collective-permute-start.3 = (bf16[96,2048]{1,0:T(8,128)(2,1)S(1)}, bf16[96,2048]{1,0:T(8,128)(2,1)S(1)}, u32[]{:S(2)}, u32[]{:S(2)}) collective-permute-start(bf16[96,2048]{1,0:T(8,128)(2,1)S(1)} %bitcast.14), channel_id=1, source_target_pairs={{0,1},{1,0},{2,3},{3,2},{4,5},{5,4},{6,7},{7,6},{8,9},{9,8},{10,11... | collective-permute-start | bytes 1179656 | tf_op jit(solution)/shard_map/ppermute | solution.py:230
  19.0 0.0 collective-permute-done.4.refs_3_
  19.0 0.1 collective-permute-start.5
  19.1 1.7 %collective-permute-done.8.refs_7_ = bf16[2,128,512]{2,1,0:T(8,128)(2,1)S(1)} collective-permute-done((bf16[2,128,512]{2,1,0:T(8,128)(2,1)S(1)}, bf16[2,128,512]{2,1,0:T(8,128)(2,1)S(1)}, u32[]{:S(2)}, u32[]{:S(2)}) %collective-permute-start.8) | collective-permute-done | bytes 262176 | tf_op jit(solution)/shard_map/ppermute | solution.py:230
  20.8 0.0 collective-permute-start.9
  20.8 1.6 %collective-permute-start.2 = (bf16[2,128,512]{2,1,0:T(8,128)(2,1)S(1)}, bf16[2,128,512]{2,1,0:T(8,128)(2,1)S(1)}, u32[]{:S(2)}, u32[]{:S(2)}) collective-permute-start(bf16[2,128,512]{2,1,0:T(8,128)(2,1)S(1)} %pad_maximum_fusion.1), channel_id=1, source_target_pairs={{0,2},{1,3},{2,0},{3,1},{4,6},{5,7},{6,4},{7,5},{8,10},{9,11},{10,... | collective-permute-start | bytes 786440 | tf_op jit(solution)/shard_map/ppermute | solution.py:230
  22.4 0.0 collective-permute-done.3.refs_2_
  22.4 0.0 collective-permute-done.9.refs_8_
  22.4 0.0 collective-permute-done.7.refs_6_
  22.4 0.0 collective-permute-done.5.refs_4_
  22.4 0.0 copy-done
  22.4 0.0 copy-done.1
  22.4 0.0 copy-done.2
  22.4 7.5 %shard_map.55 = (f32[4,768,128]{2,1,0:T(8,128)S(1)}, f32[4,768,256]{2,1,0:T(8,128)S(1)}, bf16[96,8192]{1,0:T(8,128)(2,1)}) custom-call(s32[4]{0:T(128)S(1)} %copy-done.2, s32[4,4]{1,0:T(4,128)S(1)} %copy-done.1, bf16[96,8192]{1,0:T(8,128)(2,1)S(1)} %bitcast.11, bf16[96,2048]{1,0:T(8,128)(2,1)S(1)} %bitcast.15, ...), custom_call_target="tpu_custom_call" | custom-call | flops 4831838208 | tf_op jit(solution)/shard_map/pallas_call | solution.py:205
  30.0 0.0 collective-permute-done.2.refs_1_
  30.0 0.3 collective-permute-start.10
  30.3 1.3 %collective-permute-done.10.refs_2_ = bf16[2,128,512]{2,1,0:T(8,128)(2,1)S(1)} collective-permute-done((bf16[2,128,512]{2,1,0:T(8,128)(2,1)S(1)}, bf16[2,128,512]{2,1,0:T(8,128)(2,1)S(1)}, u32[]{:S(2)}, u32[]{:S(2)}) %collective-permute-start.10) | collective-permute-done | bytes 262176 | tf_op jit(solution)/shard_map/ppermute | solution.py:230
  31.6 3.0 %shard_map.56 = bf16[96,8192]{1,0:T(8,128)(2,1)} custom-call(s32[4]{0:T(128)S(1)} %copy-done.2, s32[4,4]{1,0:T(4,128)S(1)} %copy-done.1, bf16[96,8192]{1,0:T(8,128)(2,1)S(1)} %bitcast.12, bf16[2,128,512]{2,1,0:T(8,128)(2,1)S(1)} %collective-permute-done.2.refs_1_, ...), custom_call_target="tpu_custom_call", output_to_operand_aliasing={{}: (7, {})} | custom-call | flops 805306368 | tf_op jit(solution)/shard_map/pallas_call | solution.py:205
  (4 shorter events, 0.1 us)
Async XLA Ops:
  0.0 18.5 %copy-start.3 = (bf16[1,96,2048]{2,1,0:T(8,128)(2,1)S(1)}, bf16[1,96,2048]{2,1,0:T(8,128)(2,1)}, u32[]{:S(2)}) copy-start(bf16[1,96,2048]{2,1,0:T(8,128)(2,1)} %param.6) | copy-start | bytes 1179652
  0.0 22.4 %copy-start = (bf16[1,96,8192]{2,1,0:T(8,128)(2,1)S(1)}, bf16[1,96,8192]{2,1,0:T(8,128)(2,1)}, u32[]{:S(2)}) copy-start(bf16[1,96,8192]{2,1,0:T(8,128)(2,1)} %param.5) | copy-start | bytes 4718596
  0.0 22.4 %copy-start.1 = (s32[4,4]{1,0:T(4,128)S(1)}, s32[4,4]{1,0:T(4,128)}, u32[]{:S(2)}) copy-start(s32[4,4]{1,0:T(4,128)} %holder_map.3) | copy-start | bytes 196
  0.0 22.4 %copy-start.2 = (s32[4]{0:T(128)S(1)}, s32[4]{0:T(128)}, u32[]{:S(2)}) copy-start(s32[4]{0:T(128)} %counts.3) | copy-start | bytes 52
  1.3 8.8 %collective-permute-start.6 = (bf16[1,128,512]{2,1,0:T(8,128)(2,1)S(1)}, bf16[1,128,512]{2,1,0:T(8,128)(2,1)S(1)}, u32[]{:S(2)}, u32[]{:S(2)}) collective-permute-start(bf16[1,128,512]{2,1,0:T(8,128)(2,1)S(1)} %get-tuple-element.16), channel_id=1, source_target_pairs={{0,4},{4,8},{8,12},{12,0},{1,5},{5,9},{9,13},{13,1},{2,6},{6,10},{... | collective-permute-start | bytes 393224 | tf_op jit(solution)/shard_map/ppermute | solution.py:249
  4.4 14.6 %collective-permute-start.4 = (bf16[96,2048]{1,0:T(8,128)(2,1)}, bf16[96,2048]{1,0:T(8,128)(2,1)S(1)}, u32[]{:S(2)}, u32[]{:S(2)}) collective-permute-start(bf16[96,2048]{1,0:T(8,128)(2,1)} %bitcast.13), channel_id=1, source_target_pairs={{0,2},{1,3},{2,0},{3,1},{4,6},{5,7},{6,4},{7,5},{8,10},{9,11},{10,... | collective-permute-start | bytes 1179656 | tf_op jit(solution)/shard_map/ppermute | solution.py:230
  5.9 6.8 %collective-permute-start.1 = (bf16[1,128,512]{2,1,0:T(8,128)(2,1)S(1)}, bf16[1,128,512]{2,1,0:T(8,128)(2,1)S(1)}, u32[]{:S(2)}, u32[]{:S(2)}) collective-permute-start(bf16[1,128,512]{2,1,0:T(8,128)(2,1)S(1)} %get-tuple-element.14), channel_id=1, source_target_pairs={{0,12},{4,0},{8,4},{12,8},{1,13},{5,1},{9,5},{13,9},{2,14},{6,2},{... | collective-permute-start | bytes 393224 | tf_op jit(solution)/shard_map/ppermute | solution.py:249
  8.1 10.2 %collective-permute-start = (bf16[1,128,512]{2,1,0:T(8,128)(2,1)S(1)}, bf16[1,128,512]{2,1,0:T(8,128)(2,1)S(1)}, u32[]{:S(2)}, u32[]{:S(2)}) collective-permute-start(bf16[1,128,512]{2,1,0:T(8,128)(2,1)S(1)} %get-tuple-element.15), channel_id=1, source_target_pairs={{0,8},{4,12},{8,0},{12,4},{1,9},{5,13},{9,1},{13,5},{2,10},{6,14},... | collective-permute-start | bytes 393224 | tf_op jit(solution)/shard_map/ppermute | solution.py:249
  10.1 10.7 %collective-permute-start.8 = (bf16[2,128,512]{2,1,0:T(8,128)(2,1)S(1)}, bf16[2,128,512]{2,1,0:T(8,128)(2,1)S(1)}, u32[]{:S(2)}, u32[]{:S(2)}) collective-permute-start(bf16[2,128,512]{2,1,0:T(8,128)(2,1)S(1)} %pad_maximum_fusion.2), channel_id=1, source_target_pairs={{0,2},{1,3},{2,0},{3,1},{4,6},{5,7},{6,4},{7,5},{8,10},{9,11},{10,... | collective-permute-start | bytes 786440 | tf_op jit(solution)/shard_map/ppermute | solution.py:230
  18.4 4.0 %collective-permute-start.7 = (bf16[4,128,512]{2,1,0:T(8,128)(2,1)S(1)}, bf16[4,128,512]{2,1,0:T(8,128)(2,1)S(1)}, u32[]{:S(2)}, u32[]{:S(2)}) collective-permute-start(bf16[4,128,512]{2,1,0:T(8,128)(2,1)S(1)} %pad_maximum_fusion.refs_5_), channel_id=1, source_target_pairs={{0,1},{1,0},{2,3},{3,2},{4,5},{5,4},{6,7},{7,6},{8,9},{9,8},{10,11... | collective-permute-start | bytes 1572872 | tf_op jit(solution)/shard_map/ppermute | solution.py:230
  18.5 3.9 %collective-permute-start.3 = (bf16[96,2048]{1,0:T(8,128)(2,1)S(1)}, bf16[96,2048]{1,0:T(8,128)(2,1)S(1)}, u32[]{:S(2)}, u32[]{:S(2)}) collective-permute-start(bf16[96,2048]{1,0:T(8,128)(2,1)S(1)} %bitcast.14), channel_id=1, source_target_pairs={{0,1},{1,0},{2,3},{3,2},{4,5},{5,4},{6,7},{7,6},{8,9},{9,8},{10,11... | collective-permute-start | bytes 1179656 | tf_op jit(solution)/shard_map/ppermute | solution.py:230
  19.0 3.4 %collective-permute-start.5 = (bf16[96,2048]{1,0:T(8,128)(2,1)S(1)}, bf16[96,2048]{1,0:T(8,128)(2,1)S(1)}, u32[]{:S(2)}, u32[]{:S(2)}) collective-permute-start(bf16[96,2048]{1,0:T(8,128)(2,1)S(1)} %collective-permute-done.4.refs_3_), channel_id=1, source_target_pairs={{0,1},{1,0},{2,3},{3,2},{4,5},{5,4},{6,7},{7,6},{8,9},{9,8},{10,11... | collective-permute-start | bytes 1179656 | tf_op jit(solution)/shard_map/ppermute | solution.py:230
  20.8 1.6 %collective-permute-start.9 = (bf16[2,128,512]{2,1,0:T(8,128)(2,1)S(1)}, bf16[2,128,512]{2,1,0:T(8,128)(2,1)S(1)}, u32[]{:S(2)}, u32[]{:S(2)}) collective-permute-start(bf16[2,128,512]{2,1,0:T(8,128)(2,1)S(1)} %collective-permute-done.8.refs_7_), channel_id=1, source_target_pairs={{0,1},{1,0},{2,3},{3,2},{4,5},{5,4},{6,7},{7,6},{8,9},{9,8},{10,11... | collective-permute-start | bytes 786440 | tf_op jit(solution)/shard_map/ppermute | solution.py:230
  20.8 9.2 %collective-permute-start.2 = (bf16[2,128,512]{2,1,0:T(8,128)(2,1)S(1)}, bf16[2,128,512]{2,1,0:T(8,128)(2,1)S(1)}, u32[]{:S(2)}, u32[]{:S(2)}) collective-permute-start(bf16[2,128,512]{2,1,0:T(8,128)(2,1)S(1)} %pad_maximum_fusion.1), channel_id=1, source_target_pairs={{0,2},{1,3},{2,0},{3,1},{4,6},{5,7},{6,4},{7,5},{8,10},{9,11},{10,... | collective-permute-start | bytes 786440 | tf_op jit(solution)/shard_map/ppermute | solution.py:230
  30.0 1.6 %collective-permute-start.10 = (bf16[2,128,512]{2,1,0:T(8,128)(2,1)S(1)}, bf16[2,128,512]{2,1,0:T(8,128)(2,1)S(1)}, u32[]{:S(2)}, u32[]{:S(2)}) collective-permute-start(bf16[2,128,512]{2,1,0:T(8,128)(2,1)S(1)} %collective-permute-done.2.refs_1_), channel_id=1, source_target_pairs={{0,1},{1,0},{2,3},{3,2},{4,5},{5,4},{6,7},{7,6},{8,9},{9,8},{10,11... | collective-permute-start | bytes 786440 | tf_op jit(solution)/shard_map/ppermute | solution.py:230

commit v3 on v2

--- a/solution.py
+++ b/solution.py
@@ -36,7 +36,7 @@
     me, request = lax.axis_index("tensor"), lax.axis_index("request")
     holders = holder_map.shape[1]
     tokens = q_ref.shape[0]
-    local_kv = max(job.head for job in jobs) + 1
+    local_kv = new[0].shape[1] // (2 * HD) // size if new else max(job.head for job in jobs) + 1
     heads = q_ref.shape[1] // HD // (size * local_kv)
     rows = heads * tokens
 
@@ -257,14 +257,20 @@
 
     late_away = swap(jnp.concatenate(spans[2:], axis=0), half)
 
+    nearer, away = away[:1], away[1:]
+    early_away = spread(early_away, inner)
     far = {(0, d): piece for d, piece in enumerate(spread(jnp.concatenate(spans, axis=0), inner))}
-    far |= {(0, half + d): piece for d, piece in enumerate(spread(early_away, inner))}
+    far |= {(0, half + d): piece for d, piece in enumerate(early_away)}
     jobs = [Job(d, i, True, (0,), None, None) for d, i in home]
     jobs += [Job(d, i, True, (0,), None, n) for n, (d, i) in enumerate(away)]
     state, out = attend(rules, query, new, far, jobs)
 
     late_away = after(late_away, state)
-    far = {(2, half + d): piece for d, piece in enumerate(spread(late_away, inner))}
+    last = spread(late_away, inner)
+    far = {(0, half): early_away[0], (2, half): late_away}
+    jobs = [Job(d, i, True, (0, 2), None, None) for d, i in nearer]
+    _, out = attend(rules, query, new, far, jobs, None, out)
+    far = {(2, half + d): piece for d, piece in enumerate(last)}
     jobs = [Job(d, i, False, (2,), n, None) for n, (d, i) in enumerate(away)]
     return attend(rules, query, new, far, jobs, state, out)[1][None]
 

time: 34.7 us -> 35.4 us (1.020)
  Pallas kernels: 10.5 us -> 12.5 us
  waiting for transfers between devices: 9.95 us -> 8.92 us
    pallas_call x2 -> x3, Pallas kernels: 10.5 us -> 12.5 us  [attend(): pl.pallas_call(functools.partial(attend_kernel, size, jobs, pieces, state...]
    ppermute x8, waiting for transfers between devices: 3.04 us -> 2.01 us  [swap(): return lax.ppermute(piece, 'tensor', [(i, i ^ bit) for i in range(size)])]
  transfers between devices with their start and end apart: 11 -> 11, of which waited for: 5 -> 5; matrix products, arithmetic and copies ran while one was open for 0% -> 0% of each run, Pallas kernels for 22% -> 28%
where the time goes in v3:
time: 35.4 us; the launch traced here: 35.2 us
  Pallas kernels  12.5 us (35%)
  starting transfers between devices  12.3 us (35%)
  waiting for transfers between devices  8.92 us (25%)
  local copies, waits for them, and re-layouts  1.29 us (4%)
    pallas_call x3, Pallas kernels, attend(): pl.pallas_call(functools.partial(attend_kernel, size, jobs, pieces, state...  12.5 us
    ppermute x3, waiting for transfers between devices, local(): spans.append(lax.ppermute(span_of(request + s), 'request', pairs))  6.91 us
    ppermute x8, starting transfers between devices, swap(): return lax.ppermute(piece, 'tensor', [(i, i ^ bit) for i in range(size)])  6.21 us
    ppermute x3, starting transfers between devices, local(): spans.append(lax.ppermute(span_of(request + s), 'request', pairs))  6.13 us
    ppermute x8, waiting for transfers between devices, swap(): return lax.ppermute(piece, 'tensor', [(i, i ^ bit) for i in range(size)])  2.01 us
    dynamic_slice x1, local copies, waits for them, and re-layouts, span_of(): return lax.dynamic_index_in_dim(pool, lax.rem(r, holders), 0, keepdims=True)  1.27 us
  transfers between devices with their start and end apart: 11, of which 5 were waited for; matrix products, arithmetic and copies ran while one was open for 0% of the time, Pallas kernels for 28%

profile of v3, /device:TPU:0, one launch (start us, length us, event | category | flops | bytes accessed | tf_op | source)
XLA Modules:
  0.0 35.2 jit_solution(529683342610523260)
XLA Ops:
  0.0 0.0 copy-start.1
  0.0 1.3 %dynamic-slice_bitcast_fusion.1 = (bf16[1,128,512]{2,1,0:T(8,128)(2,1)S(1)}, bf16[1,128,512]{2,1,0:T(8,128)(2,1)S(1)}, bf16[1,128,512]{2,1,0:T(8,128)(2,1)S(1)}, bf16[1,128,512]{2,1,0:T(8,128)(2,1)S(1)}) fusion(bf16[1,4,128,512]{3,2,1,0:T(8,128)(2,1)} %param.7, s32[]{:T(128)S(6)} %select_n.15, s32[]{:T(128)S(6)} %select_n.14, s32[]{:T(128)S(6)} %select_n.13, ...), kind=kLoop, calls=%fused_computation.4 | loop fusion | bytes 1048592 | tf_op jit(solution)/shard_map/jit(dynamic_index_in_dim)/dynamic_slice | solution.py:243
  1.3 3.1 %collective-permute-start.6 = (bf16[1,128,512]{2,1,0:T(8,128)(2,1)S(1)}, bf16[1,128,512]{2,1,0:T(8,128)(2,1)S(1)}, u32[]{:S(2)}, u32[]{:S(2)}) collective-permute-start(bf16[1,128,512]{2,1,0:T(8,128)(2,1)S(1)} %get-tuple-element.16), channel_id=1, source_target_pairs={{0,4},{4,8},{8,12},{12,0},{1,5},{5,9},{9,13},{13,1},{2,6},{6,10},{... | collective-permute-start | bytes 393224 | tf_op jit(solution)/shard_map/ppermute | solution.py:249
  4.4 1.5 %collective-permute-start.4 = (bf16[96,2048]{1,0:T(8,128)(2,1)}, bf16[96,2048]{1,0:T(8,128)(2,1)S(1)}, u32[]{:S(2)}, u32[]{:S(2)}) collective-permute-start(bf16[96,2048]{1,0:T(8,128)(2,1)} %bitcast.14), channel_id=1, source_target_pairs={{0,2},{1,3},{2,0},{3,1},{4,6},{5,7},{6,4},{7,5},{8,10},{9,11},{10,... | collective-permute-start | bytes 1179656 | tf_op jit(solution)/shard_map/ppermute | solution.py:230
  5.9 2.2 %collective-permute-start.1 = (bf16[1,128,512]{2,1,0:T(8,128)(2,1)S(1)}, bf16[1,128,512]{2,1,0:T(8,128)(2,1)S(1)}, u32[]{:S(2)}, u32[]{:S(2)}) collective-permute-start(bf16[1,128,512]{2,1,0:T(8,128)(2,1)S(1)} %get-tuple-element.14), channel_id=1, source_target_pairs={{0,12},{4,0},{8,4},{12,8},{1,13},{5,1},{9,5},{13,9},{2,14},{6,2},{... | collective-permute-start | bytes 393224 | tf_op jit(solution)/shard_map/ppermute | solution.py:249
  8.1 0.8 %collective-permute-start = (bf16[1,128,512]{2,1,0:T(8,128)(2,1)S(1)}, bf16[1,128,512]{2,1,0:T(8,128)(2,1)S(1)}, u32[]{:S(2)}, u32[]{:S(2)}) collective-permute-start(bf16[1,128,512]{2,1,0:T(8,128)(2,1)S(1)} %get-tuple-element.15), channel_id=1, source_target_pairs={{0,8},{4,12},{8,0},{12,4},{1,9},{5,13},{9,1},{13,5},{2,10},{6,14},... | collective-permute-start | bytes 393224 | tf_op jit(solution)/shard_map/ppermute | solution.py:249
  8.9 1.1 %collective-permute-done.6 = bf16[1,128,512]{2,1,0:T(8,128)(2,1)S(1)} collective-permute-done((bf16[1,128,512]{2,1,0:T(8,128)(2,1)S(1)}, bf16[1,128,512]{2,1,0:T(8,128)(2,1)S(1)}, u32[]{:S(2)}, u32[]{:S(2)}) %collective-permute-start.6) | collective-permute-done | bytes 131104 | tf_op jit(solution)/shard_map/ppermute | solution.py:249
  10.1 2.5 %collective-permute-start.8 = (bf16[2,128,512]{2,1,0:T(8,128)(2,1)S(1)}, bf16[2,128,512]{2,1,0:T(8,128)(2,1)S(1)}, u32[]{:S(2)}, u32[]{:S(2)}) collective-permute-start(bf16[2,128,512]{2,1,0:T(8,128)(2,1)S(1)} %pad_maximum_fusion.2), channel_id=1, source_target_pairs={{0,2},{1,3},{2,0},{3,1},{4,6},{5,7},{6,4},{7,5},{8,10},{9,11},{10,... | collective-permute-start | bytes 786440 | tf_op jit(solution)/shard_map/ppermute | solution.py:230
  12.6 0.1 collective-permute-done.1
  12.7 5.6 %collective-permute-done = bf16[1,128,512]{2,1,0:T(8,128)(2,1)S(1)} collective-permute-done((bf16[1,128,512]{2,1,0:T(8,128)(2,1)S(1)}, bf16[1,128,512]{2,1,0:T(8,128)(2,1)S(1)}, u32[]{:S(2)}, u32[]{:S(2)}) %collective-permute-start) | collective-permute-done | bytes 131104 | tf_op jit(solution)/shard_map/ppermute | solution.py:249
  18.3 0.1 pad_maximum_fusion.refs_5_
  18.4 0.1 collective-permute-start.7
  18.5 0.0 copy-done.1
  18.5 0.5 %collective-permute-start.3 = (bf16[96,2048]{1,0:T(8,128)(2,1)S(1)}, bf16[96,2048]{1,0:T(8,128)(2,1)S(1)}, u32[]{:S(2)}, u32[]{:S(2)}) collective-permute-start(bf16[96,2048]{1,0:T(8,128)(2,1)S(1)} %bitcast.15), channel_id=1, source_target_pairs={{0,1},{1,0},{2,3},{3,2},{4,5},{5,4},{6,7},{7,6},{8,9},{9,8},{10,11... | collective-permute-start | bytes 1179656 | tf_op jit(solution)/shard_map/ppermute | solution.py:230
  19.0 0.0 collective-permute-done.4.refs_3_
  19.0 0.1 collective-permute-start.5
  19.1 1.7 %collective-permute-done.8.refs_7_.refs_5_ = bf16[2,128,512]{2,1,0:T(8,128)(2,1)S(1)} collective-permute-done((bf16[2,128,512]{2,1,0:T(8,128)(2,1)S(1)}, bf16[2,128,512]{2,1,0:T(8,128)(2,1)S(1)}, u32[]{:S(2)}, u32[]{:S(2)}) %collective-permute-start.8) | collective-permute-done | bytes 262176 | tf_op jit(solution)/shard_map/ppermute | solution.py:230
  20.8 0.0 collective-permute-start.9
  20.8 1.6 %collective-permute-start.2 = (bf16[2,128,512]{2,1,0:T(8,128)(2,1)S(1)}, bf16[2,128,512]{2,1,0:T(8,128)(2,1)S(1)}, u32[]{:S(2)}, u32[]{:S(2)}) collective-permute-start(bf16[2,128,512]{2,1,0:T(8,128)(2,1)S(1)} %pad_maximum_fusion.1), channel_id=1, source_target_pairs={{0,2},{1,3},{2,0},{3,1},{4,6},{5,7},{6,4},{7,5},{8,10},{9,11},{10,... | collective-permute-start | bytes 786440 | tf_op jit(solution)/shard_map/ppermute | solution.py:230
  22.4 0.0 collective-permute-done.3.refs_2_
  22.4 0.0 collective-permute-done.9.refs_8_
  22.4 0.0 collective-permute-done.7.refs_6_
  22.4 0.0 collective-permute-done.5.refs_4_
  22.4 0.0 copy-done
  22.4 0.0 copy-done.2
  22.4 0.0 copy-done.3
  22.4 6.9 %shard_map.55 = (f32[3,768,128]{2,1,0:T(8,128)S(1)}, f32[3,768,256]{2,1,0:T(8,128)S(1)}, bf16[96,8192]{1,0:T(8,128)(2,1)}) custom-call(s32[4]{0:T(128)S(1)} %copy-done.3, s32[4,4]{1,0:T(4,128)S(1)} %copy-done.2, bf16[96,8192]{1,0:T(8,128)(2,1)S(1)} %bitcast.11, bf16[96,2048]{1,0:T(8,128)(2,1)S(1)} %bitcast.16, ...), custom_call_target="tpu_custom_call" | custom-call | flops 4328521728 | tf_op jit(solution)/shard_map/pallas_call | solution.py:205
  29.3 0.3 collective-permute-done.2.refs_6_.refs_1_
  29.6 0.0 collective-permute-start.10
  29.6 3.1 %shard_map.56.refs_5_ = bf16[96,8192]{1,0:T(8,128)(2,1)} custom-call(s32[4]{0:T(128)S(1)} %copy-done.3, s32[4,4]{1,0:T(4,128)S(1)} %copy-done.2, bf16[96,8192]{1,0:T(8,128)(2,1)S(1)} %bitcast.12, bf16[96,2048]{1,0:T(8,128)(2,1)S(1)} %bitcast.17, bf16[96,2048]{1,0:T(8,128)(2,1)S(1)} %collective-permute-done.3.refs_2_, ...), custom_call_target="tpu_custom_call", output_to_operand_aliasing={{}: (9, {})} | custom-call | flops 704643072 | tf_op jit(solution)/shard_map/pallas_call | solution.py:205
  32.7 0.0 collective-permute-done.10.refs_2_
  32.7 2.5 %shard_map.57 = bf16[96,8192]{1,0:T(8,128)(2,1)} custom-call(s32[4]{0:T(128)S(1)} %copy-done.3, s32[4,4]{1,0:T(4,128)S(1)} %copy-done.2, bf16[96,8192]{1,0:T(8,128)(2,1)S(1)} %bitcast.13, bf16[2,128,512]{2,1,0:T(8,128)(2,1)S(1)} %collective-permute-done.2.refs_6_.refs_1_, ...), custom_call_target="tpu_custom_call", output_to_operand_aliasing={{}: (7, {})} | custom-call | flops 603979776 | tf_op jit(solution)/shard_map/pallas_call | solution.py:205
  (5 shorter events, 0.1 us)
Async XLA Ops:
  0.0 18.5 %copy-start.1 = (bf16[1,96,2048]{2,1,0:T(8,128)(2,1)S(1)}, bf16[1,96,2048]{2,1,0:T(8,128)(2,1)}, u32[]{:S(2)}) copy-start(bf16[1,96,2048]{2,1,0:T(8,128)(2,1)} %param.6) | copy-start | bytes 1179652
  0.0 22.4 %copy-start = (bf16[1,96,8192]{2,1,0:T(8,128)(2,1)S(1)}, bf16[1,96,8192]{2,1,0:T(8,128)(2,1)}, u32[]{:S(2)}) copy-start(bf16[1,96,8192]{2,1,0:T(8,128)(2,1)} %param.5) | copy-start | bytes 4718596
  0.0 22.4 %copy-start.2 = (s32[4,4]{1,0:T(4,128)S(1)}, s32[4,4]{1,0:T(4,128)}, u32[]{:S(2)}) copy-start(s32[4,4]{1,0:T(4,128)} %holder_map.5) | copy-start | bytes 196
  0.0 22.4 %copy-start.3 = (s32[4]{0:T(128)S(1)}, s32[4]{0:T(128)}, u32[]{:S(2)}) copy-start(s32[4]{0:T(128)} %counts.5) | copy-start | bytes 52
  1.3 8.8 %collective-permute-start.6 = (bf16[1,128,512]{2,1,0:T(8,128)(2,1)S(1)}, bf16[1,128,512]{2,1,0:T(8,128)(2,1)S(1)}, u32[]{:S(2)}, u32[]{:S(2)}) collective-permute-start(bf16[1,128,512]{2,1,0:T(8,128)(2,1)S(1)} %get-tuple-element.16), channel_id=1, source_target_pairs={{0,4},{4,8},{8,12},{12,0},{1,5},{5,9},{9,13},{13,1},{2,6},{6,10},{... | collective-permute-start | bytes 393224 | tf_op jit(solution)/shard_map/ppermute | solution.py:249
  4.4 14.6 %collective-permute-start.4 = (bf16[96,2048]{1,0:T(8,128)(2,1)}, bf16[96,2048]{1,0:T(8,128)(2,1)S(1)}, u32[]{:S(2)}, u32[]{:S(2)}) collective-permute-start(bf16[96,2048]{1,0:T(8,128)(2,1)} %bitcast.14), channel_id=1, source_target_pairs={{0,2},{1,3},{2,0},{3,1},{4,6},{5,7},{6,4},{7,5},{8,10},{9,11},{10,... | collective-permute-start | bytes 1179656 | tf_op jit(solution)/shard_map/ppermute | solution.py:230
  5.9 6.8 %collective-permute-start.1 = (bf16[1,128,512]{2,1,0:T(8,128)(2,1)S(1)}, bf16[1,128,512]{2,1,0:T(8,128)(2,1)S(1)}, u32[]{:S(2)}, u32[]{:S(2)}) collective-permute-start(bf16[1,128,512]{2,1,0:T(8,128)(2,1)S(1)} %get-tuple-element.14), channel_id=1, source_target_pairs={{0,12},{4,0},{8,4},{12,8},{1,13},{5,1},{9,5},{13,9},{2,14},{6,2},{... | collective-permute-start | bytes 393224 | tf_op jit(solution)/shard_map/ppermute | solution.py:249
  8.1 10.2 %collective-permute-start = (bf16[1,128,512]{2,1,0:T(8,128)(2,1)S(1)}, bf16[1,128,512]{2,1,0:T(8,128)(2,1)S(1)}, u32[]{:S(2)}, u32[]{:S(2)}) collective-permute-start(bf16[1,128,512]{2,1,0:T(8,128)(2,1)S(1)} %get-tuple-element.15), channel_id=1, source_target_pairs={{0,8},{4,12},{8,0},{12,4},{1,9},{5,13},{9,1},{13,5},{2,10},{6,14},... | collective-permute-start | bytes 393224 | tf_op jit(solution)/shard_map/ppermute | solution.py:249
  10.1 10.7 %collective-permute-start.8 = (bf16[2,128,512]{2,1,0:T(8,128)(2,1)S(1)}, bf16[2,128,512]{2,1,0:T(8,128)(2,1)S(1)}, u32[]{:S(2)}, u32[]{:S(2)}) collective-permute-start(bf16[2,128,512]{2,1,0:T(8,128)(2,1)S(1)} %pad_maximum_fusion.2), channel_id=1, source_target_pairs={{0,2},{1,3},{2,0},{3,1},{4,6},{5,7},{6,4},{7,5},{8,10},{9,11},{10,... | collective-permute-start | bytes 786440 | tf_op jit(solution)/shard_map/ppermute | solution.py:230
  18.4 4.0 %collective-permute-start.7 = (bf16[4,128,512]{2,1,0:T(8,128)(2,1)S(1)}, bf16[4,128,512]{2,1,0:T(8,128)(2,1)S(1)}, u32[]{:S(2)}, u32[]{:S(2)}) collective-permute-start(bf16[4,128,512]{2,1,0:T(8,128)(2,1)S(1)} %pad_maximum_fusion.refs_5_), channel_id=1, source_target_pairs={{0,1},{1,0},{2,3},{3,2},{4,5},{5,4},{6,7},{7,6},{8,9},{9,8},{10,11... | collective-permute-start | bytes 1572872 | tf_op jit(solution)/shard_map/ppermute | solution.py:230
  18.5 3.9 %collective-permute-start.3 = (bf16[96,2048]{1,0:T(8,128)(2,1)S(1)}, bf16[96,2048]{1,0:T(8,128)(2,1)S(1)}, u32[]{:S(2)}, u32[]{:S(2)}) collective-permute-start(bf16[96,2048]{1,0:T(8,128)(2,1)S(1)} %bitcast.15), channel_id=1, source_target_pairs={{0,1},{1,0},{2,3},{3,2},{4,5},{5,4},{6,7},{7,6},{8,9},{9,8},{10,11... | collective-permute-start | bytes 1179656 | tf_op jit(solution)/shard_map/ppermute | solution.py:230
  19.0 3.4 %collective-permute-start.5 = (bf16[96,2048]{1,0:T(8,128)(2,1)S(1)}, bf16[96,2048]{1,0:T(8,128)(2,1)S(1)}, u32[]{:S(2)}, u32[]{:S(2)}) collective-permute-start(bf16[96,2048]{1,0:T(8,128)(2,1)S(1)} %collective-permute-done.4.refs_3_), channel_id=1, source_target_pairs={{0,1},{1,0},{2,3},{3,2},{4,5},{5,4},{6,7},{7,6},{8,9},{9,8},{10,11... | collective-permute-start | bytes 1179656 | tf_op jit(solution)/shard_map/ppermute | solution.py:230
  20.8 1.6 %collective-permute-start.9 = (bf16[2,128,512]{2,1,0:T(8,128)(2,1)S(1)}, bf16[2,128,512]{2,1,0:T(8,128)(2,1)S(1)}, u32[]{:S(2)}, u32[]{:S(2)}) collective-permute-start(bf16[2,128,512]{2,1,0:T(8,128)(2,1)S(1)} %collective-permute-done.8.refs_7_.refs_5_), channel_id=1, source_target_pairs={{0,1},{1,0},{2,3},{3,2},{4,5},{5,4},{6,7},{7,6},{8,9},{9,8},{10,11... | collective-permute-start | bytes 786440 | tf_op jit(solution)/shard_map/ppermute | solution.py:230
  20.8 8.8 %collective-permute-start.2 = (bf16[2,128,512]{2,1,0:T(8,128)(2,1)S(1)}, bf16[2,128,512]{2,1,0:T(8,128)(2,1)S(1)}, u32[]{:S(2)}, u32[]{:S(2)}) collective-permute-start(bf16[2,128,512]{2,1,0:T(8,128)(2,1)S(1)} %pad_maximum_fusion.1), channel_id=1, source_target_pairs={{0,2},{1,3},{2,0},{3,1},{4,6},{5,7},{6,4},{7,5},{8,10},{9,11},{10,... | collective-permute-start | bytes 786440 | tf_op jit(solution)/shard_map/ppermute | solution.py:230
  29.6 3.1 %collective-permute-start.10 = (bf16[2,128,512]{2,1,0:T(8,128)(2,1)S(1)}, bf16[2,128,512]{2,1,0:T(8,128)(2,1)S(1)}, u32[]{:S(2)}, u32[]{:S(2)}) collective-permute-start(bf16[2,128,512]{2,1,0:T(8,128)(2,1)S(1)} %collective-permute-done.2.refs_6_.refs_1_), channel_id=1, source_target_pairs={{0,1},{1,0},{2,3},{3,2},{4,5},{5,4},{6,7},{7,6},{8,9},{9,8},{10,11... | collective-permute-start | bytes 786440 | tf_op jit(solution)/shard_map/ppermute | solution.py:230
